TPU v7x, 128 devices: a whole 4x4x4 slice. The times are simulated.
128 devices in a mesh: dp: 2 (over core), expert: 64 (over y, x, z).
Axes of the slice: x: 4, y: 4, z: 4, core: 2. Of those that a mesh axis runs over, the one named last changes fastest.
Arguments:
- tokens: bfloat16 [16384, 2048], P(('dp', 'expert')), may hold values from -6 to 6
- routes: int32 [16384, 8], P(('dp', 'expert')), may hold values from 0 to 63, all different within a row; in each aligned block of 128 rows (0 to 127, 128 to 255, ...) at most 18 rows name the same one
- router_weights: bfloat16 [16384, 8], P(('dp', 'expert')), may hold values from 0.019897461 to 0.5
- w_gate: bfloat16 [64, 2048, 768], P('expert'), may hold values from -0.125 to 0.125
- w_up: bfloat16 [64, 2048, 768], P('expert'), may hold values from -0.125 to 0.125
- w_down: bfloat16 [64, 768, 2048], P('expert'), may hold values from -0.21875 to 0.21875
- out_grad: bfloat16 [16384, 2048], P(('dp', 'expert')), may hold values from -1.5 to 1.5
Outputs:
- tokens_grad: bfloat16 [16384, 2048], P(('dp', 'expert'))
- router_grad: bfloat16 [16384, 8], P(('dp', 'expert'))
- w_gate_grad: bfloat16 [64, 2048, 768], P('expert', 'dp')
- w_up_grad: bfloat16 [64, 2048, 768], P('expert', 'dp')
- w_down_grad: bfloat16 [64, 768, 2048], P('expert', 'dp')
Inputs may be any that keep to these rules, and one draw needn't show every extreme that they name: `routes`: each token names 8 different experts. Among the tokens of one device (aligned blocks of 128 tokens) no expert is named by more than 18 tokens, and some expert reaches 18 in some block of every draw.
All inputs are finite; a program needn't handle non-finite values.
Results may differ from a plain program's by a relative error of at most 0.015.
Values may be sent and summed in bfloat16 or wider, within the bound.
No kernel may reach another device: no remote copies, remote signals or barrier semaphores. Data moves between devices by JAX's collectives and lax.ppermute only.
A program may use at most 192 MiB of HBM per device.

v0:
```python
import jax
import jax.numpy as jnp
from jax import lax
from jax.sharding import PartitionSpec as P


def contract_rows(left, right):
    return lax.dot_general(
        left, right, (((0,), (0,)), ((), ())), preferred_element_type=jnp.float32
    )


def body(tokens, routes, router_weights, w_gate, w_up, w_down, out_grad):
    token_count, width = tokens.shape
    chosen = routes.shape[1]
    experts = lax.axis_size("expert")
    capacity = max(2, 9 * token_count * chosen // (8 * experts))
    gate_local = w_gate[0]
    up_local = w_up[0]
    down_local = w_down[0]
    hidden_width = gate_local.shape[1]
    flat_experts = routes.reshape(-1)
    row_count = flat_experts.shape[0]
    one_hot = (flat_experts[:, None] == jnp.arange(experts, dtype=jnp.int32)[None, :]).astype(
        jnp.int32
    )
    earlier = jnp.cumsum(one_hot, axis=0) - one_hot
    rank_in = jnp.sum(earlier * one_hot, axis=1)
    slot_of = flat_experts * capacity + rank_in
    slot_total = experts * capacity
    source_of = (
        jnp.zeros((slot_total,), jnp.int32).at[slot_of].set(jnp.arange(row_count, dtype=jnp.int32))
    )
    filled = jnp.zeros((slot_total,), jnp.bfloat16).at[slot_of].set(1)
    token_of = source_of // chosen
    send_x = jnp.take(tokens, token_of, axis=0).reshape(experts, capacity, width)
    send_dy = jnp.take(out_grad, token_of, axis=0).reshape(experts, capacity, width)
    send_g = (jnp.take(router_weights.reshape(-1), source_of) * filled).reshape(experts, capacity)
    rows_x = lax.all_to_all(send_x, "expert", split_axis=0, concat_axis=0, tiled=True)
    rows_dy = lax.all_to_all(send_dy, "expert", split_axis=0, concat_axis=0, tiled=True)
    rows_g = lax.all_to_all(send_g, "expert", split_axis=0, concat_axis=0, tiled=True)
    source_count, slot_count, row_width = rows_x.shape
    flat_x = rows_x.reshape(source_count * slot_count, row_width)
    flat_dy = rows_dy.reshape(source_count * slot_count, row_width)
    weight = rows_g.reshape(source_count * slot_count, 1).astype(jnp.float32)
    pre_gate = jnp.dot(flat_x, gate_local, preferred_element_type=jnp.float32)
    pre_up = jnp.dot(flat_x, up_local, preferred_element_type=jnp.float32)
    sigmoid_gate = jax.nn.sigmoid(pre_gate)
    active = pre_gate * sigmoid_gate
    hidden = active * pre_up
    back_hidden = lax.dot_general(
        flat_dy, down_local, (((1,), (1,)), ((), ())), preferred_element_type=jnp.float32
    )
    router_part = jnp.sum(back_hidden * hidden, axis=1).astype(jnp.bfloat16)
    scaled_back = weight * back_hidden
    grad_gate = (
        scaled_back * pre_up * sigmoid_gate * (1.0 + pre_gate * (1.0 - sigmoid_gate))
    ).astype(jnp.bfloat16)
    grad_up = (scaled_back * active).astype(jnp.bfloat16)
    scaled_hidden = (weight * hidden).astype(jnp.bfloat16)
    token_part = lax.dot_general(
        grad_gate, gate_local, (((1,), (1,)), ((), ())), preferred_element_type=jnp.float32
    )
    token_part = token_part + lax.dot_general(
        grad_up, up_local, (((1,), (1,)), ((), ())), preferred_element_type=jnp.float32
    )
    token_part = token_part.astype(jnp.bfloat16)
    back_part = lax.all_to_all(
        token_part.reshape(source_count, slot_count, row_width),
        "expert",
        split_axis=0,
        concat_axis=0,
        tiled=True,
    )
    back_router = lax.all_to_all(
        router_part.reshape(source_count, slot_count),
        "expert",
        split_axis=0,
        concat_axis=0,
        tiled=True,
    )
    both_grads = jnp.concatenate([grad_gate, grad_up], axis=1).reshape(
        source_count, slot_count, 2 * hidden_width
    )
    back_part, back_router, both_grads, scaled_hidden, rows_x, rows_dy = (
        back_part,
        back_router,
        both_grads,
        scaled_hidden.reshape(source_count, slot_count, hidden_width),
        rows_x,
        rows_dy,
    )
    part_rows = back_part.reshape(slot_total, width)
    picked = (
        jnp.take(part_rows, slot_of, axis=0).reshape(token_count, chosen, width).astype(jnp.float32)
    )
    tokens_grad = jnp.sum(picked, axis=1).astype(jnp.bfloat16)
    router_grad = jnp.take(back_router.reshape(-1), slot_of).reshape(token_count, chosen)
    slot_x = rows_x.reshape(slot_total, width)
    slot_dy = rows_dy.reshape(slot_total, width)
    both_flat = both_grads.reshape(slot_total, 2 * hidden_width)
    hidden_flat = scaled_hidden.reshape(slot_total, hidden_width)
    columns = slot_x
    summed = lax.psum_scatter(
        contract_rows(columns, both_flat), "dp", scatter_dimension=0, tiled=True
    )
    columns = hidden_flat
    down_summed = lax.psum_scatter(
        contract_rows(columns, slot_dy), "dp", scatter_dimension=0, tiled=True
    )
    w_gate_grad = summed[:, :hidden_width].astype(jnp.bfloat16)[None]
    w_up_grad = summed[:, hidden_width:].astype(jnp.bfloat16)[None]
    w_down_grad = down_summed.astype(jnp.bfloat16)[None]
    return (tokens_grad, router_grad, w_gate_grad, w_up_grad, w_down_grad)


def solution(mesh):
    placed = (
        P(("dp", "expert"), None),
        P(("dp", "expert"), None),
        P(("dp", "expert"), None),
        P("expert", None, None),
        P("expert", None, None),
        P("expert", None, None),
        P(("dp", "expert"), None),
    )
    return jax.shard_map(
        body,
        mesh=mesh,
        in_specs=placed,
        out_specs=(
            P(("dp", "expert"), None),
            P(("dp", "expert"), None),
            P("expert", "dp", None),
            P("expert", "dp", None),
            P("expert", "dp", None),
        ),
        check_vma=False,
    )
```

profile of v0, /device:TPU:50, one launch (start us, length us, event | category | flops | bytes accessed | tf_op | source)
XLA Modules:
  0.0 521.1 jit_solution(13854219815118869137)
XLA Ops:
  7.2 0.0 copy-start
  7.2 0.9 copy.20
  8.1 0.1 eq.26
  8.2 0.1 reshape.142
  8.3 0.7 fusion.21
  9.0 31.1 %reduce-window.6 = s32[64,8,128]{2,1,0:T(8,128)S(1)} reduce-window(s32[64,8,128]{2,1,0:T(8,128)} %fusion.21, s32[]{:T(128)} %constant.56.clone.1), window={size=1x1x128 pad=0_0x0_0x127_0}, to_apply=%region_0.0 | reduce-window | flops 8323072 | bytes 524292 | tf_op jit(solution)/shard_map/reduce-window
  40.1 0.8 slice.28
  41.0 1.1 copy.23
  42.1 0.7 copy.24
  42.8 1.6 broadcast_add_fusion
  44.4 0.1 mul.67
  44.5 1.0 fusion.20
  45.5 4.3 scatter_custom_fusion
  49.9 0.8 copy.25
  50.7 0.1 reshape.144
  50.8 7.3 %gather_fusion = bf16[1152]{0:T(1024)(128)(2,1)S(1)} fusion(bf16[1024]{0:T(1024)(128)(2,1)S(1)} %reshape.144, s32[2048]{0:T(1024)S(1)} %pad_clamp_fusion.1), kind=kCustom, calls=%fused_computation.2 | custom fusion | bytes 9216 | tf_op jit(solution)/shard_map/jit(_take)/gather | solution.py:38
  58.1 7.6 %scatter_custom_fusion.1 = bf16[1152]{0:T(1024)(128)(2,1)S(1)} fusion(s32[1024]{0:T(1024)S(1)} %bitcast.56, bf16[1024]{0:T(1024)(128)(2,1)S(1)} %broadcast.81, bf16[]{:T(256)} %constant.78.clone.1), kind=kCustom, calls=%fused_computation.68 | custom fusion | bytes 2306 | tf_op jit(solution)/shard_map/scatter | solution.py:34
  65.7 0.8 all_to_all.25
  66.5 11.3 %all-to-all-start = ((bf16[64,1,18]{2,1,0:T(2,128)(2,1)}), bf16[64,1,18]{2,1,0:T(2,128)(2,1)S(1)}, u32[]{:S(2)}, u32[]{:S(2)}) async-start(bf16[64,1,18]{2,1,0:T(2,128)(2,1)} %all_to_all.25), calls=%async_computation | async-start | bytes 65536 | tf_op jit(solution)/shard_map/all_to_all | solution.py:41
  77.8 11.8 %gather_fusion.3 = bf16[1152,2048]{1,0:T(8,128)(2,1)} fusion(bf16[128,2048]{1,0:T(8,128)(2,1)} %param.15, s32[2048]{0:T(1024)S(1)} %pad_clamp_fusion), kind=kCustom, calls=%fused_computation.clone | custom fusion | bytes 9441792 | tf_op jit(solution)/shard_map/jit(_take)/gather | solution.py:37
  89.6 11.8 %gather_fusion.4 = bf16[1152,2048]{1,0:T(8,128)(2,1)} fusion(bf16[128,2048]{1,0:T(8,128)(2,1)} %param.9, s32[2048]{0:T(1024)S(1)} %pad_clamp_fusion), kind=kCustom, calls=%fused_computation.1.clone | custom fusion | bytes 9441792 | tf_op jit(solution)/shard_map/jit(_take)/gather | solution.py:36
  101.3 8.6 %broadcast_select_fusion.1 = (bf16[1152,2048]{1,0:T(8,128)(2,1)}, bf16[1152,2048]{1,0:T(8,128)(2,1)}) fusion(bf16[1152,2048]{1,0:T(8,128)(2,1)} %gather_fusion.3, pred[1152]{0:T(1024)(128)(4,1)S(1)} %get-tuple-element.18, bf16[1152,2048]{1,0:T(8,128)(2,1)} %gather_fusion.4), kind=kLoop, calls=%fused_computation.9 | loop fusion | flops 4718592 | bytes 18875520 | tf_op jit(solution)/shard_map/jit(_take)/select_n | solution.py:37
  110.0 7.6 %reshape.147 = bf16[64,18,2048]{2,1,0:T(8,128)(2,1)} reshape(bf16[1152,2048]{1,0:T(8,128)(2,1)} %get-tuple-element.26) | data formatting | bytes 9437184 | tf_op jit(solution)/shard_map/reshape | solution.py:36
  117.5 0.0 all-to-all-done
  117.5 10.5 %all-to-all-start.2 = ((bf16[64,18,2048]{2,1,0:T(8,128)(2,1)}), bf16[64,18,2048]{2,1,0:T(8,128)(2,1)}, u32[]{:S(2)}, u32[]{:S(2)}) async-start(bf16[64,18,2048]{2,1,0:T(8,128)(2,1)} %reshape.147), calls=%async_computation.2 | async-start | bytes 12582912 | tf_op jit(solution)/shard_map/all_to_all | solution.py:39
  128.0 7.6 %reshape.145 = bf16[64,18,2048]{2,1,0:T(8,128)(2,1)} reshape(bf16[1152,2048]{1,0:T(8,128)(2,1)} %get-tuple-element.25) | data formatting | bytes 9437184 | tf_op jit(solution)/shard_map/reshape | solution.py:37
  135.6 78.0 %all-to-all-done.2 = bf16[64,18,2048]{2,1,0:T(8,128)(2,1)} async-done(((bf16[64,18,2048]{2,1,0:T(8,128)(2,1)}), bf16[64,18,2048]{2,1,0:T(8,128)(2,1)}, u32[]{:S(2)}, u32[]{:S(2)}) %all-to-all-start.2) | async-done | bytes 4718624 | tf_op jit(solution)/shard_map/all_to_all | solution.py:39
  213.7 11.0 %all-to-all-start.1 = ((bf16[64,18,2048]{2,1,0:T(8,128)(2,1)}), bf16[64,18,2048]{2,1,0:T(8,128)(2,1)}, u32[]{:S(2)}, u32[]{:S(2)}) async-start(bf16[64,18,2048]{2,1,0:T(8,128)(2,1)} %reshape.145), calls=%async_computation.1 | async-start | bytes 12582912 | tf_op jit(solution)/shard_map/all_to_all | solution.py:40
  224.7 0.3 reduce-scatter.5.cloned.1.call-start
  225.0 0.1 convert_reduce_fusion
  225.1 0.1 reshape.152
  225.2 7.7 %reshape.148 = bf16[1152,2048]{1,0:T(8,128)(2,1)} reshape(bf16[64,18,2048]{2,1,0:T(8,128)(2,1)} %all-to-all-done.2) | data formatting | bytes 9437184 | tf_op jit(solution)/shard_map/reshape | solution.py:43
  232.9 9.6 %fusion.11 = f32[1152,768]{0,1:T(8,128)} fusion(bf16[1152,2048]{1,0:T(8,128)(2,1)} %reshape.148, bf16[1,2048,768]{2,1,0:T(8,128)(2,1)} %param.13), kind=kOutput, calls=%fused_computation.27 | convolution fusion | flops 3623878656 | bytes 11403264 | tf_op jit(solution)/shard_map/dot_general | solution.py:47
  242.5 6.4 %fusion.8 = f32[1152,768]{0,1:T(8,128)} fusion(bf16[1152,2048]{1,0:T(8,128)(2,1)S(1)} %copy-done.1, bf16[1,2048,768]{2,1,0:T(8,128)(2,1)S(1)} %copy-done), kind=kOutput, calls=%fused_computation.24 | convolution fusion | flops 3623878656 | bytes 11403264 | tf_op jit(solution)/shard_map/dot_general | solution.py:46
  248.9 61.3 %all-to-all-done.1 = bf16[64,18,2048]{2,1,0:T(8,128)(2,1)} async-done(((bf16[64,18,2048]{2,1,0:T(8,128)(2,1)}), bf16[64,18,2048]{2,1,0:T(8,128)(2,1)}, u32[]{:S(2)}, u32[]{:S(2)}) %all-to-all-start.1) | async-done | bytes 4718624 | tf_op jit(solution)/shard_map/all_to_all | solution.py:40
  310.2 8.2 %reshape.146 = bf16[1152,2048]{1,0:T(8,128)(2,1)} reshape(bf16[64,18,2048]{2,1,0:T(8,128)(2,1)} %all-to-all-done.1) | data formatting | bytes 9437184 | tf_op jit(solution)/shard_map/reshape | solution.py:44
  318.4 11.3 %fusion.15 = f32[768,2048]{1,0:T(8,128)} fusion(bf16[1152,2048]{1,0:T(8,128)(2,1)} %reshape.146, f32[1152]{0:T(1024)S(1)} %reshape.152, f32[1152,768]{0,1:T(8,128)} %fusion.11, f32[1152,768]{0,1:T(8,128)} %fusion.8), kind=kOutput, calls=%fused_computation.31 | convolution fusion | flops 3630071808 | bytes 18092544 | tf_op jit(solution)/shard_map/dot_general | solution.py:8
  329.7 0.0 reduce-scatter.5.cloned.1.call-update
  329.7 0.0 reduce-scatter.3.cloned.1.call-start
  329.8 10.8 %multiply_reduce_fusion = (bf16[1152]{0:T(1024)(128)(2,1)S(1)}, bf16[1152,768]{0,1:T(8,128)(2,1)S(1)}, bf16[1152,768]{0,1:T(8,128)(2,1)S(1)}) fusion(f32[1152,768]{0,1:T(8,128)} %fusion.11, f32[1152,768]{0,1:T(8,128)} %fusion.8, f32[1152]{0:T(1024)S(1)} %reshape.152, bf16[1152,2048]{1,0:T(8,128)(2,1)} %reshape.146, bf16[1,768,2048]{2,1,0:T(8,128)(2,1)} %param.14), kind=kOutput, calls=%fused_computation.17 | convolution fusion | flops 3638918144 | bytes 18488064 | tf_op jit(solution)/shard_map/dot_general | solution.py:51
  340.6 1.3 copy-done.3
  341.9 0.6 copy-done.4
  342.5 13.6 %fusion.1 = f32[2048,1536]{1,0:T(8,128)} fusion(bf16[1152,2048]{1,0:T(8,128)(2,1)} %reshape.148, bf16[1152,768]{0,1:T(8,128)(2,1)S(1)} %get-tuple-element.22, bf16[1152,768]{0,1:T(8,128)(2,1)S(1)} %get-tuple-element.21), kind=kOutput, calls=%fused_computation.12 | convolution fusion | flops 7254835200 | bytes 20840448 | tf_op jit(solution)/shard_map/dot_general | solution.py:8
  356.0 0.0 reduce-scatter.3.cloned.1.call-update
  356.1 0.8 convert_element_type.63
  356.8 10.9 %all-to-all-start.4 = ((bf16[64,1,18]{2,1,0:T(2,128)(2,1)}), bf16[64,1,18]{2,1,0:T(2,128)(2,1)S(1)}, u32[]{:S(2)}, u32[]{:S(2)}) async-start(bf16[64,1,18]{2,1,0:T(2,128)(2,1)} %convert_element_type.63), calls=%async_computation.4 | async-start | bytes 65536 | tf_op jit(solution)/shard_map/all_to_all | solution.py:75
  367.7 0.0 copy-start.2
  367.7 5.6 %fusion.6 = f32[1152,2048]{1,0:T(8,128)S(1)} fusion(bf16[1152,768]{0,1:T(8,128)(2,1)} %copy-done.3, bf16[1,2048,768]{2,1,0:T(8,128)(2,1)S(1)} %copy-done), kind=kOutput, calls=%fused_computation.22 | convolution fusion | flops 3623878656 | bytes 14352384 | tf_op jit(solution)/shard_map/dot_general | solution.py:61
  373.4 5.7 %add_convert_fusion = bf16[1152,2048]{1,0:T(8,128)(2,1)} fusion(f32[1152,2048]{1,0:T(8,128)S(1)} %fusion.6, bf16[1152,768]{0,1:T(8,128)(2,1)S(1)} %copy-done.5, bf16[1,2048,768]{2,1,0:T(8,128)(2,1)S(1)} %copy-done.2), kind=kOutput, calls=%fused_computation.7 | convolution fusion | flops 3628597248 | bytes 19070976 | tf_op jit(solution)/shard_map/dot_general | solution.py:64
  379.1 7.6 %reshape.149 = bf16[64,18,2048]{2,1,0:T(8,128)(2,1)} reshape(bf16[1152,2048]{1,0:T(8,128)(2,1)} %add_convert_fusion) | data formatting | bytes 9437184 | tf_op jit(solution)/shard_map/reshape | solution.py:69
  386.7 10.9 %all-to-all-start.3 = ((bf16[64,18,2048]{2,1,0:T(8,128)(2,1)}), bf16[64,18,2048]{2,1,0:T(8,128)(2,1)}, u32[]{:S(2)}, u32[]{:S(2)}) async-start(bf16[64,18,2048]{2,1,0:T(8,128)(2,1)} %reshape.149), calls=%async_computation.3 | async-start | bytes 12582912 | tf_op jit(solution)/shard_map/all_to_all | solution.py:68
  397.6 0.1 reduce_sum.35
  397.7 0.1 reduce.2
  397.8 0.1 reshape.151
  397.9 6.8 %gather_fusion.2 = bf16[1024]{0:T(1024)(128)(2,1)S(1)} fusion(bf16[1152]{0:T(1024)(128)(2,1)S(1)} %reshape.151, s32[1024]{0:T(1024)S(1)} %broadcast_clamp_fusion), kind=kCustom, calls=%fused_computation.4 | custom fusion | bytes 8192 | tf_op jit(solution)/shard_map/jit(_take)/gather | solution.py:98
  404.7 0.1 gather.23
  404.9 0.7 copy.28
  405.5 75.6 %all-to-all-done.3 = bf16[64,18,2048]{2,1,0:T(8,128)(2,1)} async-done(((bf16[64,18,2048]{2,1,0:T(8,128)(2,1)}), bf16[64,18,2048]{2,1,0:T(8,128)(2,1)}, u32[]{:S(2)}, u32[]{:S(2)}) %all-to-all-start.3) | async-done | bytes 4718624 | tf_op jit(solution)/shard_map/all_to_all | solution.py:68
  481.2 7.7 %reshape.150 = bf16[1152,2048]{1,0:T(8,128)(2,1)} reshape(bf16[64,18,2048]{2,1,0:T(8,128)(2,1)} %all-to-all-done.3) | data formatting | bytes 9437184 | tf_op jit(solution)/shard_map/reshape | solution.py:93
  488.9 11.8 %gather_fusion.1 = bf16[1024,2048]{1,0:T(8,128)(2,1)} fusion(bf16[1152,2048]{1,0:T(8,128)(2,1)} %reshape.150, s32[1024]{0:T(1024)S(1)} %broadcast_clamp_fusion), kind=kCustom, calls=%fused_computation.3 | custom fusion | bytes 8392704 | tf_op jit(solution)/shard_map/jit(_take)/gather | solution.py:95
  500.6 5.1 fusion
  505.8 3.3 convert_bitcast_fusion
  509.0 3.2 convert.6
  512.2 1.9 slice_bitcast_fusion
  (24 shorter events, 0.2 us)
Async XLA Ops:
  7.2 235.4 %copy-start = (bf16[1,2048,768]{2,1,0:T(8,128)(2,1)S(1)}, bf16[1,2048,768]{2,1,0:T(8,128)(2,1)}, u32[]{:S(2)}) copy-start(bf16[1,2048,768]{2,1,0:T(8,128)(2,1)} %param.12) | copy-start | bytes 9437188
  66.5 51.1 %all-to-all-start = ((bf16[64,1,18]{2,1,0:T(2,128)(2,1)}), bf16[64,1,18]{2,1,0:T(2,128)(2,1)S(1)}, u32[]{:S(2)}, u32[]{:S(2)}) async-start(bf16[64,1,18]{2,1,0:T(2,128)(2,1)} %all_to_all.25), calls=%async_computation | async-start | bytes 65536 | tf_op jit(solution)/shard_map/all_to_all | solution.py:41
  117.5 96.1 %all-to-all-start.2 = ((bf16[64,18,2048]{2,1,0:T(8,128)(2,1)}), bf16[64,18,2048]{2,1,0:T(8,128)(2,1)}, u32[]{:S(2)}, u32[]{:S(2)}) async-start(bf16[64,18,2048]{2,1,0:T(8,128)(2,1)} %reshape.147), calls=%async_computation.2 | async-start | bytes 12582912 | tf_op jit(solution)/shard_map/all_to_all | solution.py:39
  213.7 96.6 %all-to-all-start.1 = ((bf16[64,18,2048]{2,1,0:T(8,128)(2,1)}), bf16[64,18,2048]{2,1,0:T(8,128)(2,1)}, u32[]{:S(2)}, u32[]{:S(2)}) async-start(bf16[64,18,2048]{2,1,0:T(8,128)(2,1)} %reshape.145), calls=%async_computation.1 | async-start | bytes 12582912 | tf_op jit(solution)/shard_map/all_to_all | solution.py:40
  224.7 281.1 %reduce-scatter.5.cloned.1.call-start = ((), (), s32[]{:S(2)}) async-start(), calls=%async_computation.8 | async-start | bytes 9437184 | tf_op jit(solution)/shard_map/reduce_scatter | solution.py:108
  232.9 9.6 %copy-start.1 = (bf16[1152,2048]{1,0:T(8,128)(2,1)S(1)}, bf16[1152,2048]{1,0:T(8,128)(2,1)}, u32[]{:S(2)}) copy-start(bf16[1152,2048]{1,0:T(8,128)(2,1)} %reshape.148) | copy-start | bytes 14155780
  329.7 179.3 %reduce-scatter.3.cloned.1.call-start = ((), (), s32[]{:S(2)}) async-start(), calls=%async_computation.7 | async-start | bytes 18874368 | tf_op jit(solution)/shard_map/reduce_scatter | solution.py:104
  340.6 1.3 copy-start.3
  340.6 1.8 copy-start.4
  356.8 29.9 %all-to-all-start.4 = ((bf16[64,1,18]{2,1,0:T(2,128)(2,1)}), bf16[64,1,18]{2,1,0:T(2,128)(2,1)S(1)}, u32[]{:S(2)}, u32[]{:S(2)}) async-start(bf16[64,1,18]{2,1,0:T(2,128)(2,1)} %convert_element_type.63), calls=%async_computation.4 | async-start | bytes 65536 | tf_op jit(solution)/shard_map/all_to_all | solution.py:75
  367.7 5.6 %copy-start.2 = (bf16[1,2048,768]{2,1,0:T(8,128)(2,1)S(1)}, bf16[1,2048,768]{2,1,0:T(8,128)(2,1)}, u32[]{:S(2)}) copy-start(bf16[1,2048,768]{2,1,0:T(8,128)(2,1)} %param.13) | copy-start | bytes 9437188
  367.7 5.6 %copy-start.5 = (bf16[1152,768]{0,1:T(8,128)(2,1)S(1)}, bf16[1152,768]{0,1:T(8,128)(2,1)}, u32[]{:S(2)}) copy-start(bf16[1152,768]{0,1:T(8,128)(2,1)} %copy-done.4) | copy-start | bytes 5308420
  386.7 94.5 %all-to-all-start.3 = ((bf16[64,18,2048]{2,1,0:T(8,128)(2,1)}), bf16[64,18,2048]{2,1,0:T(8,128)(2,1)}, u32[]{:S(2)}, u32[]{:S(2)}) async-start(bf16[64,18,2048]{2,1,0:T(8,128)(2,1)} %reshape.149), calls=%async_computation.3 | async-start | bytes 12582912 | tf_op jit(solution)/shard_map/all_to_all | solution.py:68
Sparse Core Ops, SparseCore 0:
  329.9 19.0 reduce-scatter.4
  356.2 25.9 reduce-scatter.2
where the time goes:
time: 530 us; the launch traced here: 521 us
  waiting for transfers between devices  215 us (41%)
  local copies, waits for them, and re-layouts  119 us (22%)
  matrix products  63 us (12%)
  other arithmetic  55 us (10%)
  starting transfers between devices  54.9 us (10%)
  between operations  14.5 us (3%)
    all_to_all x1, waiting for transfers between devices, body(): lax.all_to_all(send_x, 'expert', split_axis=0, concat_axis=0, tiled=True)  78 us
    all_to_all x1, waiting for transfers between devices, body(): lax.all_to_all(token_part.reshape(source_count, slot_count, row_width), '...  75.6 us
    all_to_all x1, waiting for transfers between devices, body(): lax.all_to_all(send_dy, 'expert', split_axis=0, concat_axis=0, tiled=True)  61.3 us
    another operation x4, other arithmetic  35.9 us
    dot_general x2, matrix products, contract_rows(): lax.dot_general(left, right, (((0,), (0,)), ((), ())), preferred_element_...  24.9 us
    gather x1, local copies, waits for them, and re-layouts, body(): jnp.take(tokens, token_of, axis=0).reshape(experts, capacity, width)  11.8 us
    gather x1, local copies, waits for them, and re-layouts, body(): jnp.take(part_rows, slot_of, axis=0).reshape(token_count, chosen, width)  11.8 us
    gather x1, local copies, waits for them, and re-layouts, body(): jnp.take(out_grad, token_of, axis=0).reshape(experts, capacity, width)  11.8 us
  transfers between devices with their start and end apart: 7, of which 3 were waited for; matrix products, arithmetic and copies ran while one was open for 29% of the time, Pallas kernels for 0%

commit v1 on v0

v1 whole, which is shorter than its diff:
```python
import functools

import jax
import jax.numpy as jnp
from jax import lax
from jax.experimental import pallas as pl
from jax.experimental.pallas import tpu as pltpu
from jax.sharding import PartitionSpec as P

F32, BF16 = jnp.float32, jnp.bfloat16
SLOTS = 16
EXTRA = 2
GROUP = 16
ROWS = GROUP * (SLOTS + EXTRA)
MAIN = GROUP * SLOTS
LANES = 128
MIB = 1 << 20


def iota(shape, axis):
    return lax.broadcasted_iota(jnp.int32, shape, axis)


def dot(a, b):
    return jnp.dot(a, b, preferred_element_type=F32)


def dot_rows(a, b):
    return lax.dot_general(a, b, (((0,), (0,)), ((), ())), preferred_element_type=F32)


def unit(n, m):
    return (iota((n, m), 0) == iota((n, m), 1)).astype(BF16)


def spread_rows(block):
    wide = jnp.broadcast_to(block[:, None, :], (GROUP, 16, LANES))
    return wide.reshape(MAIN, LANES)


def chunk_rows(value, pieces):
    width = value.shape[1] // pieces
    return jnp.concatenate([value[:, i * width : (i + 1) * width] for i in range(pieces)], axis=0)


def chunk_columns(value, pieces):
    height = value.shape[0] // pieces
    return jnp.concatenate([value[i * height : (i + 1) * height] for i in range(pieces)], axis=1)


def tile_rows(ref, blocks):
    return jnp.concatenate(
        [ref[:, j * 16 : (j + 1) * 16, :].reshape(MAIN, LANES) for j in blocks], axis=1
    )


def put_tiles(ref, value, first):
    for j in range(value.shape[1] // LANES):
        at = (first + j) * 16
        ref[:, at : at + 16, :] = value[:, j * LANES : (j + 1) * LANES].reshape(GROUP, 16, LANES)


def route_tables(routes_ref, weights_ref, rank_ref, weight_ref):
    tokens = routes_ref.shape[0]
    experts = iota((tokens, LANES), 1)
    mask = jnp.zeros((tokens, LANES), F32)
    weight = jnp.zeros((tokens, LANES), F32)
    for k in range(routes_ref.shape[1]):
        hit = routes_ref[:, k : k + 1] == experts
        mask = mask + hit.astype(F32)
        if weights_ref is not None:
            weight = weight + jnp.where(hit, weights_ref[:, k : k + 1].astype(F32), 0.0)
    mask = mask.astype(BF16)
    earlier = (iota((tokens, tokens), 0) < iota((tokens, tokens), 1)).astype(BF16)
    same = unit(tokens, tokens)
    rank = dot_rows(mask, earlier)
    rank_ref[...] = jnp.where(dot_rows(mask, same) > 0.5, rank, -1.0)
    if weights_ref is not None:
        weight_ref[...] = dot_rows(weight.astype(BF16), same)


def slot_masks(ranks):
    wide = spread_rows(ranks)
    place = iota((MAIN, LANES), 0) % 16
    main = wide == place.astype(F32)
    over = wide == (SLOTS + place // 8).astype(F32)
    return wide, place, main, over


def over_pieces(over, place):
    return jnp.concatenate(
        [jnp.where(over & (place % 8 == c), 1.0, 0.0).astype(BF16) for c in range(8)], axis=1
    )


def pack_kernel(scalars, routes_ref, weights_ref, rows_ref, send_ref, *rest):
    rank_out = None if scalars else rest[0]
    rank_ref, weight_ref = rest[-2:]
    step = pl.program_id(0)

    @pl.when(step == 0)
    def _():
        route_tables(routes_ref, weights_ref if scalars else None, rank_ref, weight_ref)

    here = pl.ds(pl.multiple_of(step * GROUP, GROUP), GROUP)
    ranks = rank_ref[here, :]
    wide, place, main, over = slot_masks(ranks)
    rows = rows_ref[...]
    put_tiles(send_ref, dot(main.astype(F32).astype(BF16), rows).astype(BF16), 0)
    put_tiles(send_ref, dot(over_pieces(over, place), chunk_rows(rows, 8)).astype(BF16), 16)
    if scalars:
        weight = spread_rows(weight_ref[here, :])
        first = jnp.where(main, weight, 0.0).astype(BF16)
        second = jnp.where(wide == (SLOTS + place).astype(F32), weight, 0.0).astype(BF16)
        low = (iota((LANES, LANES), 1) < 64).astype(F32)
        tile = dot(first, low.astype(BF16)) + dot(second, (1.0 - low).astype(BF16))
        put_tiles(send_ref, tile.astype(BF16), 18)
    else:
        rank_out[...] = ranks


def over_select():
    shape = (8 * EXTRA * GROUP, MAIN)
    row, col = iota(shape, 0), iota(shape, 1)
    c, r, s = row // (EXTRA * GROUP), (row // GROUP) % EXTRA, row % GROUP
    return (col == s * 16 + r * 8 + c).astype(F32).astype(BF16)


def unpack(recv_ref):
    main = tile_rows(recv_ref, range(16))
    pieces = dot(over_select(), tile_rows(recv_ref, (16, 17))).astype(BF16)
    return jnp.concatenate([main, chunk_columns(pieces, 8)], axis=0)


def forward_kernel(recv_ref, gate_ref, up_ref, x_ref, act_ref, slope_ref, hidden_ref):
    x = unpack(recv_ref)
    x_ref[...] = x
    pre_gate = dot(x, gate_ref[...])
    pre_up = dot(x, up_ref[...])
    sig = jax.nn.sigmoid(pre_gate)
    active = pre_gate * sig
    act_ref[...] = active
    slope_ref[...] = pre_up * sig * (1.0 + pre_gate * (1.0 - sig))
    hidden_ref[...] = active * pre_up


def backward_kernel(
    recv_ref,
    act_ref,
    slope_ref,
    hidden_ref,
    down_ref,
    both_ref,
    send_ref,
    dy_ref,
    gate_grads_ref,
    up_grads_ref,
    sh_ref,
):
    dy = unpack(recv_ref)
    dy_ref[...] = dy
    tile = tile_rows(recv_ref, (18,))
    shape = (EXTRA * GROUP, MAIN)
    row = iota(shape, 0)
    pick = (iota(shape, 1) == (row % GROUP) * 16 + row // GROUP).astype(F32).astype(BF16)
    weight = jnp.concatenate(
        [tile[:, 0:1].astype(F32), dot(pick, tile)[:, 64:65]], axis=0
    )
    back = dot(dy, down_ref[...])
    hidden = hidden_ref[...]
    router = jnp.sum(back * hidden, axis=1, keepdims=True)
    scaled = weight * back
    sh_ref[...] = (weight * hidden).astype(BF16)
    gate_grads = (scaled * slope_ref[...]).astype(BF16)
    up_grads = (scaled * act_ref[...]).astype(BF16)
    gate_grads_ref[...] = gate_grads
    up_grads_ref[...] = up_grads
    grads = jnp.concatenate([gate_grads, up_grads], axis=1)
    part = dot(grads, both_ref[...]).astype(BF16)
    put_tiles(send_ref, part[:MAIN], 0)
    pieces = chunk_rows(part[MAIN:], 8)
    put_tiles(send_ref, dot_rows(over_select(), pieces).astype(BF16), 16)
    router_wide = jnp.broadcast_to(router, (ROWS, LANES))
    second = dot_rows(pick, router_wide[MAIN:].astype(BF16))
    lane = iota((MAIN, LANES), 1)
    put_tiles(send_ref, jnp.where(lane < 64, router_wide[:MAIN], second).astype(BF16), 18)


def combine_kernel(recv_ref, rank_ref, routes_ref, grad_ref, router_ref, total_ref, value_ref):
    step = pl.program_id(0)
    tokens = routes_ref.shape[0]

    @pl.when(step == 0)
    def _():
        total_ref[...] = jnp.zeros_like(total_ref)

    wide, place, main, over = slot_masks(rank_ref[...])
    total_ref[...] += dot_rows(main.astype(F32).astype(BF16), tile_rows(recv_ref, range(16)))
    pieces = dot_rows(over_pieces(over, place), tile_rows(recv_ref, (16, 17)))
    total_ref[...] += chunk_columns(pieces, 8)
    tile = tile_rows(recv_ref, (18,)).astype(F32)
    value = jnp.where(main, tile[:, 0:1], 0.0) + jnp.where(
        wide == (SLOTS + place).astype(F32), tile[:, 64:65], 0.0
    )
    here = pl.ds(pl.multiple_of(step * GROUP, GROUP), GROUP)
    value_ref[here, :] = jnp.sum(value.reshape(GROUP, 16, LANES), axis=1)

    @pl.when(step == pl.num_programs(0) - 1)
    def _():
        grad_ref[...] = total_ref[...].astype(BF16)
        by_token = dot_rows(value_ref[...].astype(BF16), unit(value_ref.shape[0], LANES))
        experts = iota((tokens, LANES), 1)
        lane = iota(router_ref.shape, 1)
        out = jnp.zeros(router_ref.shape, F32)
        for k in range(router_ref.shape[1]):
            picked = jnp.where(routes_ref[:, k : k + 1] == experts, by_token, 0.0)
            out = jnp.where(lane == k, jnp.sum(picked, axis=1, keepdims=True), out)
        router_ref[...] = out.astype(BF16)


def whole(shape):
    return pl.BlockSpec(shape, lambda i: (0,) * len(shape), pipeline_mode=pl.Buffered(1))


def params(mib):
    return pltpu.CompilerParams(
        vmem_limit_bytes=mib * MIB, dimension_semantics=("arbitrary",)
    )


def cost(flops, size):
    return pl.CostEstimate(flops=flops, bytes_accessed=size, transcendentals=0)


def pack(scalars, experts, routes, weights, rows):
    tokens, width = rows.shape
    high = 16 * (width // LANES) + 32 + 16 * scalars
    outs = [jax.ShapeDtypeStruct((experts, high, LANES), BF16)]
    out_specs = [pl.BlockSpec((GROUP, high, LANES), lambda i: (i, 0, 0))]
    if not scalars:
        outs.append(jax.ShapeDtypeStruct((experts, tokens), F32))
        out_specs.append(pl.BlockSpec((GROUP, tokens), lambda i: (i, 0)))
    return pl.pallas_call(
        functools.partial(pack_kernel, scalars),
        grid=(experts // GROUP,),
        in_specs=[whole(routes.shape), whole(weights.shape), whole(rows.shape)],
        out_specs=out_specs,
        out_shape=outs,
        scratch_shapes=[pltpu.VMEM((LANES, tokens), F32)] * 2,
        compiler_params=params(32),
        cost_estimate=cost(4 * experts * 18 * tokens * width, 2 * experts * high * LANES),
        name="pack_rows",
    )(routes, weights, rows)


def forward(recv, gate, up):
    sources, high, _ = recv.shape
    width, units = gate.shape
    total = sources * (SLOTS + EXTRA)
    by_rows = lambda n: pl.BlockSpec((ROWS, n), lambda i: (i, 0))
    return pl.pallas_call(
        forward_kernel,
        grid=(sources // GROUP,),
        in_specs=[
            pl.BlockSpec((GROUP, high, LANES), lambda i: (i, 0, 0)),
            whole(gate.shape),
            whole(up.shape),
        ],
        out_specs=[by_rows(width), by_rows(units), by_rows(units), by_rows(units)],
        out_shape=[
            jax.ShapeDtypeStruct((total, width), BF16),
            jax.ShapeDtypeStruct((total, units), F32),
            jax.ShapeDtypeStruct((total, units), F32),
            jax.ShapeDtypeStruct((total, units), F32),
        ],
        compiler_params=params(48),
        cost_estimate=cost(4 * total * width * units, 30 * MIB),
        name="expert_forward",
    )(recv, gate, up)


def backward(recv, act, slope, hidden, down, both):
    sources, high, _ = recv.shape
    width, units = down.shape
    total = sources * (SLOTS + EXTRA)
    by_rows = lambda n: pl.BlockSpec((ROWS, n), lambda i: (i, 0))
    by_source = pl.BlockSpec((GROUP, high, LANES), lambda i: (i, 0, 0))
    return pl.pallas_call(
        backward_kernel,
        grid=(sources // GROUP,),
        in_specs=[
            by_source,
            by_rows(units),
            by_rows(units),
            by_rows(units),
            whole(down.shape),
            whole(both.shape),
        ],
        out_specs=[by_source, by_rows(width), by_rows(units), by_rows(units), by_rows(units)],
        out_shape=[
            jax.ShapeDtypeStruct(recv.shape, BF16),
            jax.ShapeDtypeStruct((total, width), BF16),
            jax.ShapeDtypeStruct((total, units), BF16),
            jax.ShapeDtypeStruct((total, units), BF16),
            jax.ShapeDtypeStruct((total, units), BF16),
        ],
        compiler_params=params(48),
        cost_estimate=cost(6 * total * width * units, 40 * MIB),
        name="expert_backward",
    )(recv, act, slope, hidden, down, both)


def combine(recv, ranks, routes, width):
    experts, high, _ = recv.shape
    tokens, chosen = routes.shape
    return pl.pallas_call(
        combine_kernel,
        grid=(experts // GROUP,),
        in_specs=[
            pl.BlockSpec((GROUP, high, LANES), lambda i: (i, 0, 0)),
            pl.BlockSpec((GROUP, tokens), lambda i: (i, 0)),
            whole(routes.shape),
        ],
        out_specs=[
            pl.BlockSpec((tokens, width), lambda i: (0, 0)),
            pl.BlockSpec((tokens, chosen), lambda i: (0, 0)),
        ],
        out_shape=[
            jax.ShapeDtypeStruct((tokens, width), BF16),
            jax.ShapeDtypeStruct((tokens, chosen), BF16),
        ],
        scratch_shapes=[pltpu.VMEM((tokens, width), F32), pltpu.VMEM((experts, tokens), F32)],
        compiler_params=params(32),
        cost_estimate=cost(4 * experts * 18 * tokens * width, 2 * experts * high * LANES),
        name="combine_parts",
    )(recv, ranks, routes)


def exchange(value):
    return lax.all_to_all(value, "expert", split_axis=0, concat_axis=0, tiled=True)


def summed_halves(left, right):
    half = left.shape[1] // 2
    me = lax.axis_index("dp")
    theirs = lax.dynamic_slice_in_dim(left, (1 - me) * half, half, axis=1)
    mine = lax.dynamic_slice_in_dim(left, me * half, half, axis=1)
    arrived = lax.ppermute(dot_rows(theirs, right).astype(BF16), "dp", [(0, 1), (1, 0)])
    return (dot_rows(mine, right) + arrived.astype(F32)).astype(BF16)


def body(tokens, routes, router_weights, w_gate, w_up, w_down, out_grad):
    experts = lax.axis_size("expert")
    width = tokens.shape[1]
    gate, up, down = w_gate[0], w_up[0], w_down[0]
    units = gate.shape[1]
    send_x, ranks = pack(False, experts, routes, router_weights, tokens)
    recv_x = exchange(send_x)
    _, routes_b, out_grad, gate_b, up_b, down_b = lax.optimization_barrier(
        (ranks, routes, out_grad, gate, up, down)
    )
    send_dy = pack(True, experts, routes_b, router_weights, out_grad)[0]
    both = jnp.concatenate([gate_b.T, up_b.T], axis=0)
    down_t = down_b.T
    recv_dy = exchange(send_dy)
    x, act, slope, hidden = forward(recv_x, gate, up)
    send_back, dy, gate_grads, up_grads, scaled_hidden = backward(recv_dy, act, slope, hidden, down_t, both)
    recv_back = exchange(send_back)
    gate_grad = summed_halves(x, gate_grads)
    up_grad = summed_halves(x, up_grads)
    down_grad = summed_halves(scaled_hidden, dy)
    tokens_grad, router_grad = combine(recv_back, ranks, routes, width)
    return (
        tokens_grad,
        router_grad,
        gate_grad[None],
        up_grad[None],
        down_grad[None],
    )


def solution(mesh):
    placed = (
        P(("dp", "expert"), None),
        P(("dp", "expert"), None),
        P(("dp", "expert"), None),
        P("expert", None, None),
        P("expert", None, None),
        P("expert", None, None),
        P(("dp", "expert"), None),
    )
    return jax.shard_map(
        body,
        mesh=mesh,
        in_specs=placed,
        out_specs=(
            P(("dp", "expert"), None),
            P(("dp", "expert"), None),
            P("expert", "dp", None),
            P("expert", "dp", None),
            P("expert", "dp", None),
        ),
        check_vma=False,
    )
```

time: 530 us -> 256 us (0.48); the launches traced: 521 us -> 253 us
  waiting for transfers between devices: 215 us -> 115 us
  local copies, waits for them, and re-layouts: 119 us -> 23.8 us
  other arithmetic: 55 us -> 6.63 us
  Pallas kernels: 0 us -> 45.7 us
  matrix products: 63 us -> 31.9 us
  starting transfers between devices: 54.9 us -> 29.8 us
  between operations: 14.5 us -> 0.76 us
    all_to_all x5 -> x3, waiting for transfers between devices: 215 us -> 115 us  [exchange(): lax.all_to_all(value, 'expert', split_axis=0, concat_axis=0, tiled=True)]
    gather x6 -> x0, local copies, waits for them, and re-layouts: 49.5 us -> none  [the longest x1 11.8 us: body(): jnp.take(tokens, token_of, axis=0).reshape(experts, capacity, width)]
    reshape x9 -> x0, local copies, waits for them, and re-layouts: 46.7 us -> none  [the longest x1 8.15 us: body(): flat_dy = rows_dy.reshape(source_count * slot_count, row_width)]
    pallas_call x0 -> x5, Pallas kernels: none -> 45.7 us  [the longest x1 21.8 us: backward(): pl.pallas_call(backward_kernel, grid=(sources // GROUP,), in_specs=[by_so...]
    another operation x4 -> x0, other arithmetic: 35.9 us -> none
    dot_general x7 -> x6, matrix products: 63 us -> 31.9 us  [dot_rows(): lax.dot_general(a, b, (((0,), (0,)), ((), ())), preferred_element_type=F32)]
    all_to_all x5 -> x3, starting transfers between devices: 54.5 us -> 29.3 us  [exchange(): lax.all_to_all(value, 'expert', split_axis=0, concat_axis=0, tiled=True)]
    unnamed x15 -> x30, local copies, waits for them, and re-layouts: 4.25 us -> 23.7 us
  transfers between devices with their start and end apart: 7 -> 6, of which waited for: 3 -> 3; matrix products, arithmetic and copies ran while one was open for 29% -> 20% of each run, Pallas kernels for 0% -> 6%
where the time goes in v1:
time: 256 us; the launch traced here: 253 us
  waiting for transfers between devices  115 us (45%)
  Pallas kernels  45.7 us (18%)
  matrix products  31.9 us (12%)
  starting transfers between devices  29.8 us (12%)
  local copies, waits for them, and re-layouts  23.8 us (9%)
  other arithmetic  6.63 us (3%)
    all_to_all x3, waiting for transfers between devices, exchange(): lax.all_to_all(value, 'expert', split_axis=0, concat_axis=0, tiled=True)  115 us
    dot_general x6, matrix products, dot_rows(): lax.dot_general(a, b, (((0,), (0,)), ((), ())), preferred_element_type=F32)  31.9 us
    all_to_all x3, starting transfers between devices, exchange(): lax.all_to_all(value, 'expert', split_axis=0, concat_axis=0, tiled=True)  29.3 us
    unnamed x30, local copies, waits for them, and re-layouts  23.7 us
    pallas_call x1, Pallas kernels, backward(): pl.pallas_call(backward_kernel, grid=(sources // GROUP,), in_specs=[by_so...  21.8 us
    pallas_call x1, Pallas kernels, forward(): pl.pallas_call(forward_kernel, grid=(sources // GROUP,), in_specs=[pl.Blo...  12.4 us
    concatenate x1, other arithmetic, body(): both = jnp.concatenate([gate_b.T, up_b.T], axis=0)  6.63 us
    pallas_call x1, Pallas kernels, combine(): pl.pallas_call(combine_kernel, grid=(experts // GROUP,), in_specs=[pl.Blo...  5.9 us
  transfers between devices with their start and end apart: 6, of which 3 were waited for; matrix products, arithmetic and copies ran while one was open for 20% of the time, Pallas kernels for 6%

profile of v1, /device:TPU:50, one launch (start us, length us, event | category | flops | bytes accessed | tf_op | source)
XLA Modules:
  0.0 253.2 jit_solution(12411759676269048228)
XLA Ops:
  0.6 0.8 copy.12.routes_ref
  1.4 0.8 copy.13.weights_ref
  2.2 0.0 copy-start.4
  2.2 1.0 copy-done.4
  3.3 2.7 %pack_rows.2 = (bf16[64,288,128]{2,1,0:T(8,128)(2,1)S(1)}, f32[64,128]{1,0:T(8,128)S(1)}) custom-call(s32[128,8]{1,0:T(8,128)S(1)} %copy.12.routes_ref, bf16[128,8]{1,0:T(8,128)(2,1)S(1)} %copy.13.weights_ref, bf16[128,2048]{1,0:T(8,128)(2,1)S(1)} %copy-done.4), custom_call_target="tpu_custom_call" | custom-call | flops 1207959552 | bytes 4718592 | tf_op jit(solution)/shard_map/pack_rows/pallas_call | solution.py:243
  6.0 0.0 copy-start.1
  6.0 2.1 copy-done.1
  8.1 0.0 copy-start.2
  8.1 11.4 %all-to-all-start.1 = ((bf16[64,288,128]{2,1,0:T(8,128)(2,1)}), bf16[64,288,128]{2,1,0:T(8,128)(2,1)}, u32[]{:S(2)}, u32[]{:S(2)}) async-start(bf16[64,288,128]{2,1,0:T(8,128)(2,1)} %copy-done.1), calls=%async_computation.1 | async-start | bytes 9437184 | tf_op jit(solution)/shard_map/all_to_all | solution.py:340
  19.5 0.0 copy-done.2
  19.5 3.0 %copy.14 = bf16[1,2048,768]{1,2,0:T(8,128)(2,1)} copy(bf16[1,2048,768]{2,1,0:T(8,128)(2,1)S(1)} %copy-done.2) | data formatting | bytes 6291456 | tf_op args[3]
  22.5 4.7 %copy.15 = bf16[1,2048,768]{1,2,0:T(8,128)(2,1)} copy(bf16[1,2048,768]{2,1,0:T(8,128)(2,1)} %param.11) | data formatting | bytes 6291456 | tf_op args[4]
  27.2 0.0 copy-start.9
  27.2 4.7 %copy.16 = bf16[1,768,2048]{1,2,0:T(8,128)(2,1)} copy(bf16[1,768,2048]{2,1,0:T(8,128)(2,1)} %param.12) | data formatting | bytes 6291456 | tf_op args[5]
  31.9 0.0 copy-done.9
  31.9 0.1 copy.17.routes_ref
  32.0 0.0 copy-start.3
  32.0 1.0 copy-done.3
  33.1 2.9 %pack_rows.3 = bf16[64,304,128]{2,1,0:T(8,128)(2,1)S(1)} custom-call(s32[128,8]{1,0:T(8,128)S(1)} %copy.17.routes_ref, bf16[128,8]{1,0:T(8,128)(2,1)S(1)} %copy.13.weights_ref, bf16[128,2048]{1,0:T(8,128)(2,1)S(1)} %copy-done.3), custom_call_target="tpu_custom_call" | custom-call | flops 1207959552 | bytes 4980736 | tf_op jit(solution)/shard_map/pack_rows/pallas_call | solution.py:243
  36.0 0.0 copy-start
  36.0 2.3 copy-done
  38.3 42.5 %all-to-all-done.1.recv_ref = bf16[64,288,128]{2,1,0:T(8,128)(2,1)} async-done(((bf16[64,288,128]{2,1,0:T(8,128)(2,1)}), bf16[64,288,128]{2,1,0:T(8,128)(2,1)}, u32[]{:S(2)}, u32[]{:S(2)}) %all-to-all-start.1) | async-done | bytes 4718624 | tf_op jit(solution)/shard_map/all_to_all | solution.py:340
  80.8 8.3 %all-to-all-start = ((bf16[64,304,128]{2,1,0:T(8,128)(2,1)}), bf16[64,304,128]{2,1,0:T(8,128)(2,1)}, u32[]{:S(2)}, u32[]{:S(2)}) async-start(bf16[64,304,128]{2,1,0:T(8,128)(2,1)} %copy-done), calls=%async_computation | async-start | bytes 9961472 | tf_op jit(solution)/shard_map/all_to_all | solution.py:340
  89.1 6.6 %pad_maximum_fusion.both_ref = bf16[1536,2048]{1,0:T(8,128)(2,1)} fusion(bf16[768,2048]{1,0:T(8,128)(2,1)} %bitcast.22, bf16[768,2048]{1,0:T(8,128)(2,1)} %bitcast.21), kind=kLoop, calls=%fused_computation | loop fusion | flops 12582912 | bytes 12582912 | tf_op jit(solution)/shard_map/concatenate | solution.py:363
  95.7 12.4 %expert_forward.1 = (bf16[1152,2048]{1,0:T(8,128)(2,1)}, f32[1152,768]{1,0:T(8,128)}, f32[1152,768]{1,0:T(8,128)}, f32[1152,768]{1,0:T(8,128)}) custom-call(bf16[64,288,128]{2,1,0:T(8,128)(2,1)} %all-to-all-done.1.recv_ref, bf16[2048,768]{1,0:T(8,128)(2,1)S(1)} %bitcast.20, bf16[2048,768]{1,0:T(8,128)(2,1)} %bitcast.25), custom_call_target="tpu_custom_call" | custom-call | flops 7247757312 | bytes 31457280 | tf_op jit(solution)/shard_map/expert_forward/pallas_call | solution.py:261
  108.1 46.0 %all-to-all-done.recv_ref = bf16[64,304,128]{2,1,0:T(8,128)(2,1)} async-done(((bf16[64,304,128]{2,1,0:T(8,128)(2,1)}), bf16[64,304,128]{2,1,0:T(8,128)(2,1)}, u32[]{:S(2)}, u32[]{:S(2)}) %all-to-all-start) | async-done | bytes 4980768 | tf_op jit(solution)/shard_map/all_to_all | solution.py:340
  154.1 21.8 %expert_backward.1 = (bf16[64,304,128]{2,1,0:T(8,128)(2,1)}, bf16[1152,2048]{1,0:T(8,128)(2,1)}, bf16[1152,768]{1,0:T(8,128)(2,1)S(1)}, bf16[1152,768]{1,0:T(8,128)(2,1)S(1)}, bf16[1152,768]{1,0:T(8,128)(2,1)S(1)}) custom-call(bf16[64,304,128]{2,1,0:T(8,128)(2,1)} %all-to-all-done.recv_ref, f32[1152,768]{1,0:T(8,128)} %get-tuple-element.27.act_ref, ...), custom_call_target="tpu_custom_call" | custom-call | flops 10871635968 | bytes 41943040 | tf_op jit(solution)/shard_map/expert_backward/pallas_call | solution.py:288
  175.9 0.0 copy-start.5
  175.9 1.3 copy-done.5
  177.2 0.0 copy-start.8
  177.2 1.2 copy-done.8
  178.4 9.7 %all-to-all-start.2 = ((bf16[64,304,128]{2,1,0:T(8,128)(2,1)}), bf16[64,304,128]{2,1,0:T(8,128)(2,1)}, u32[]{:S(2)}, u32[]{:S(2)}) async-start(bf16[64,304,128]{2,1,0:T(8,128)(2,1)} %get-tuple-element.33), calls=%async_computation.2 | async-start | bytes 9961472 | tf_op jit(solution)/shard_map/all_to_all | solution.py:340
  188.1 0.0 copy-start.6
  188.1 5.7 %fusion.11 = bf16[1024,768]{1,0:T(8,128)(2,1)} fusion(bf16[1152,768]{1,0:T(8,128)(2,1)} %copy-done.8, bf16[1152,2048]{1,0:T(8,128)(2,1)} %get-tuple-element.36, s32[]{:T(128)S(6)} %select_n.15), kind=kOutput, calls=%fused_computation.14 | convolution fusion | flops 1812725760 | bytes 5701636 | tf_op jit(solution)/shard_map/dot_general | solution.py:29
  193.9 0.0 collective-permute-start.1
  193.9 0.0 copy-done.6
  193.9 5.1 %fusion.8 = bf16[1024,768]{1,0:T(8,128)(2,1)} fusion(bf16[1152,768]{1,0:T(8,128)(2,1)S(1)} %copy-done.6, bf16[1152,2048]{1,0:T(8,128)(2,1)} %get-tuple-element.36, s32[]{:T(128)S(6)} %select_n.15), kind=kOutput, calls=%fused_computation.13 | convolution fusion | flops 1812725760 | bytes 5701636 | tf_op jit(solution)/shard_map/dot_general | solution.py:29
  199.0 0.5 collective-permute-start
  199.6 5.7 %convolution_convert_fusion = bf16[384,2048]{1,0:T(8,128)(2,1)} fusion(bf16[1152,2048]{1,0:T(8,128)(2,1)} %get-tuple-element.40, bf16[1152,768]{1,0:T(8,128)(2,1)S(1)} %get-tuple-element.39, s32[]{:T(128)S(6)} %select_n.17), kind=kOutput, calls=%fused_computation.4 | convolution fusion | flops 1812725760 | bytes 7176196 | tf_op jit(solution)/shard_map/dot_general | solution.py:29
  205.3 0.0 collective-permute-start.2
  205.3 0.0 copy-start.7
  205.3 0.0 collective-permute-done.1
  205.3 0.0 slice-start
  205.3 6.2 %fusion.15 = bf16[1,1024,768]{2,1,0:T(8,128)(2,1)} fusion(bf16[1024,768]{1,0:T(8,128)(2,1)} %collective-permute-done.1, bf16[1152,768]{1,0:T(8,128)(2,1)} %copy-done.8, bf16[1152,2048]{1,0:T(8,128)(2,1)} %get-tuple-element.36, s32[]{:T(128)S(6)} %select_n.14), kind=kOutput, calls=%fused_computation.16 | convolution fusion | flops 1814298624 | bytes 7274500 | tf_op jit(solution)/shard_map/dot_general | solution.py:29
  211.5 0.0 slice-start.1
  211.5 0.0 collective-permute-done
  211.5 0.0 copy-done.7
  211.5 5.6 %fusion.14 = bf16[1,1024,768]{2,1,0:T(8,128)(2,1)} fusion(bf16[1024,768]{1,0:T(8,128)(2,1)} %collective-permute-done, bf16[1152,768]{1,0:T(8,128)(2,1)S(1)} %copy-done.7, bf16[1152,2048]{1,0:T(8,128)(2,1)} %get-tuple-element.36, s32[]{:T(128)S(6)} %select_n.14), kind=kOutput, calls=%fused_computation.15 | convolution fusion | flops 1814298624 | bytes 7274500 | tf_op jit(solution)/shard_map/dot_general | solution.py:29
  217.2 0.0 collective-permute-done.2
  217.2 0.0 slice-done
  217.2 0.0 slice-done.1
  217.2 3.4 %fusion.16 = bf16[1,384,2048]{2,1,0:T(8,128)(2,1)} fusion(bf16[384,2048]{1,0:T(8,128)(2,1)S(1)} %collective-permute-done.2, bf16[1152,2048]{1,0:T(8,128)(2,1)S(1)} %bitcast.24, bf16[1152,768]{1,0:T(8,128)(2,1)S(1)} %get-tuple-element.39, s32[]{:T(128)S(6)} %select_n.16), kind=kOutput, calls=%fused_computation.17 | convolution fusion | flops 1814298624 | bytes 8749060 | tf_op jit(solution)/shard_map/dot_general | solution.py:29
  220.6 26.1 %all-to-all-done.2.recv_ref = bf16[64,304,128]{2,1,0:T(8,128)(2,1)} async-done(((bf16[64,304,128]{2,1,0:T(8,128)(2,1)}), bf16[64,304,128]{2,1,0:T(8,128)(2,1)}, u32[]{:S(2)}, u32[]{:S(2)}) %all-to-all-start.2) | async-done | bytes 4980768 | tf_op jit(solution)/shard_map/all_to_all | solution.py:340
  246.7 5.9 %combine_parts.1 = (bf16[128,2048]{1,0:T(8,128)(2,1)}, bf16[128,8]{1,0:T(8,128)(2,1)S(1)}) custom-call(bf16[64,304,128]{2,1,0:T(8,128)(2,1)} %all-to-all-done.2.recv_ref, f32[64,128]{1,0:T(8,128)S(1)} %get-tuple-element.23.rank_ref, s32[128,8]{1,0:T(8,128)S(1)} %copy.12.routes_ref), custom_call_target="tpu_custom_call" | custom-call | flops 1207959552 | bytes 4980736 | tf_op jit(solution)/shard_map/combine_parts/pallas_call | solution.py:316
  252.6 0.7 copy.22
  (1 shorter events, 0.0 us)
Async XLA Ops:
  2.2 1.0 copy-start.4
  6.0 2.1 copy-start.1
  8.1 11.4 %copy-start.2 = (bf16[1,2048,768]{2,1,0:T(8,128)(2,1)S(1)}, bf16[1,2048,768]{2,1,0:T(8,128)(2,1)}, u32[]{:S(2)}) copy-start(bf16[1,2048,768]{2,1,0:T(8,128)(2,1)} %param.10) | copy-start | bytes 9437188
  8.1 72.6 %all-to-all-start.1 = ((bf16[64,288,128]{2,1,0:T(8,128)(2,1)}), bf16[64,288,128]{2,1,0:T(8,128)(2,1)}, u32[]{:S(2)}, u32[]{:S(2)}) async-start(bf16[64,288,128]{2,1,0:T(8,128)(2,1)} %copy-done.1), calls=%async_computation.1 | async-start | bytes 9437184 | tf_op jit(solution)/shard_map/all_to_all | solution.py:340
  27.2 4.7 %copy-start.9 = (s32[128,8]{0,1:T(8,128)S(1)}, s32[128,8]{0,1:T(8,128)}, u32[]{:S(2)}) copy-start(s32[128,8]{0,1:T(8,128)} %param.8) | copy-start | bytes 12292
  32.0 1.0 copy-start.3
  36.0 2.3 copy-start
  80.8 73.3 %all-to-all-start = ((bf16[64,304,128]{2,1,0:T(8,128)(2,1)}), bf16[64,304,128]{2,1,0:T(8,128)(2,1)}, u32[]{:S(2)}, u32[]{:S(2)}) async-start(bf16[64,304,128]{2,1,0:T(8,128)(2,1)} %copy-done), calls=%async_computation | async-start | bytes 9961472 | tf_op jit(solution)/shard_map/all_to_all | solution.py:340
  175.9 1.3 copy-start.5
  177.2 1.2 copy-start.8
  178.4 68.2 %all-to-all-start.2 = ((bf16[64,304,128]{2,1,0:T(8,128)(2,1)}), bf16[64,304,128]{2,1,0:T(8,128)(2,1)}, u32[]{:S(2)}, u32[]{:S(2)}) async-start(bf16[64,304,128]{2,1,0:T(8,128)(2,1)} %get-tuple-element.33), calls=%async_computation.2 | async-start | bytes 9961472 | tf_op jit(solution)/shard_map/all_to_all | solution.py:340
  188.1 5.8 %copy-start.6 = (bf16[1152,768]{1,0:T(8,128)(2,1)S(1)}, bf16[1152,768]{1,0:T(8,128)(2,1)}, u32[]{:S(2)}) copy-start(bf16[1152,768]{1,0:T(8,128)(2,1)} %copy-done.5) | copy-start | bytes 5308420
  193.9 11.4 %collective-permute-start.1 = (bf16[1024,768]{1,0:T(8,128)(2,1)}, bf16[1024,768]{1,0:T(8,128)(2,1)}, u32[]{:S(2)}, u32[]{:S(2)}) collective-permute-start(bf16[1024,768]{1,0:T(8,128)(2,1)} %fusion.11), channel_id=1, source_target_pairs={{0,64},{64,0},{1,65},{65,1},{2,66},{66,2},{3,67},{67,3},{4,68},{68... | collective-permute-start | bytes 4718600 | tf_op jit(solution)/shard_map/ppermute | solution.py:348
  199.0 12.5 %collective-permute-start = (bf16[1024,768]{1,0:T(8,128)(2,1)}, bf16[1024,768]{1,0:T(8,128)(2,1)}, u32[]{:S(2)}, u32[]{:S(2)}) collective-permute-start(bf16[1024,768]{1,0:T(8,128)(2,1)} %fusion.8), channel_id=1, source_target_pairs={{0,64},{64,0},{1,65},{65,1},{2,66},{66,2},{3,67},{67,3},{4,68},{68... | collective-permute-start | bytes 4718600 | tf_op jit(solution)/shard_map/ppermute | solution.py:348
  205.3 11.9 %collective-permute-start.2 = (bf16[384,2048]{1,0:T(8,128)(2,1)}, bf16[384,2048]{1,0:T(8,128)(2,1)S(1)}, u32[]{:S(2)}, u32[]{:S(2)}) collective-permute-start(bf16[384,2048]{1,0:T(8,128)(2,1)} %convolution_convert_fusion), channel_id=1, source_target_pairs={{0,64},{64,0},{1,65},{65,1},{2,66},{66,2},{3,67},{67,3},{4,68},{68... | collective-permute-start | bytes 4718600 | tf_op jit(solution)/shard_map/ppermute | solution.py:348
  205.3 6.3 %copy-start.7 = (bf16[1152,768]{1,0:T(8,128)(2,1)S(1)}, bf16[1152,768]{1,0:T(8,128)(2,1)}, u32[]{:S(2)}) copy-start(bf16[1152,768]{1,0:T(8,128)(2,1)} %copy-done.5) | copy-start | bytes 5308420
  205.3 11.9 %slice-start = ((s8[4718592]{0:T(1024)(128)(4,1)}), s8[4194304]{0:T(1024)(128)(4,1)S(1)}, s32[]{:S(2)}) async-start(s8[4718592]{0:T(1024)(128)(4,1)} %bitcast.23), calls=%async_computation.3 | async-start | bytes 8388608
  211.5 5.7 %slice-start.1 = ((s8[4718592]{0:T(1024)(128)(4,1)}), s8[524288]{0:T(1024)(128)(4,1)S(1)}, s32[]{:S(2)}) async-start(s8[4718592]{0:T(1024)(128)(4,1)} %bitcast.23), calls=%async_computation.4 | async-start | bytes 1048576

commit v2 on v0

v2 whole, which is shorter than its diff:
```python
import functools

import jax
import jax.numpy as jnp
from jax import lax
from jax.experimental import pallas as pl
from jax.experimental.pallas import tpu as pltpu
from jax.sharding import PartitionSpec as P

F32, BF16 = jnp.float32, jnp.bfloat16
PARTS = 2
SLOTS = 8
GROUP = 16
MAIN = GROUP * SLOTS
ROWS = MAIN + GROUP
FINE = GROUP * 16
TILES = 9
STEP = 2
LANES = 128
MIB = 1 << 20


def iota(shape, axis):
    return lax.broadcasted_iota(jnp.int32, shape, axis)


def dot(a, b):
    return jnp.dot(a, b, preferred_element_type=F32)


def dot_columns(a, b):
    return lax.dot_general(a, b, (((1,), (1,)), ((), ())), preferred_element_type=F32)


def dot_rows(a, b):
    return lax.dot_general(a, b, (((0,), (0,)), ((), ())), preferred_element_type=F32)


def ones_where(mask):
    return jnp.where(mask, 1.0, 0.0).astype(BF16)


def unit(n, m):
    return ones_where(iota((n, m), 0) == iota((n, m), 1))


def spread_rows(block):
    wide = jnp.broadcast_to(block[:, None, :], (GROUP, 16, LANES))
    return wide.reshape(FINE, LANES)


def chunk_rows(value, pieces):
    width = value.shape[1] // pieces
    return jnp.concatenate([value[:, i * width : (i + 1) * width] for i in range(pieces)], axis=0)


def chunk_columns(value, pieces):
    height = value.shape[0] // pieces
    return jnp.concatenate([value[i * height : (i + 1) * height] for i in range(pieces)], axis=1)


def get_tiles(ref, group, first, count):
    here = slice(group * GROUP, (group + 1) * GROUP)
    return jnp.concatenate(
        [
            ref[here, j * 16 : (j + 1) * 16, :].reshape(FINE, LANES)
            for j in range(first, first + count)
        ],
        axis=1,
    )


def put_tiles(ref, group, first, value):
    here = slice(group * GROUP, (group + 1) * GROUP)
    for j in range(value.shape[1] // LANES):
        at = (first + j) * 16
        ref[here, at : at + 16, :] = value[:, j * LANES : (j + 1) * LANES].reshape(
            GROUP, 16, LANES
        )


def fine_of(pieces):
    row, col = iota((FINE, FINE), 0), iota((FINE, FINE), 1)
    s, q = row // 16, row % 16
    rows = 16 // pieces
    return ones_where(col == (q % pieces) * (FINE // pieces) + s * rows + q // pieces)


def rows_of(pieces):
    row, col = iota((FINE, FINE), 0), iota((FINE, FINE), 1)
    rows = 16 // pieces
    c, s, r = row // (FINE // pieces), (row // rows) % GROUP, row % rows
    return ones_where(col == s * 16 + r * pieces + c)


def unpack(ref, group, first):
    main = dot(rows_of(2), get_tiles(ref, group, first, TILES - 1)).astype(BF16)
    last = dot(rows_of(16), get_tiles(ref, group, first + TILES - 1, 1)).astype(BF16)
    return jnp.concatenate([chunk_columns(main, 2), chunk_columns(last, 16)], axis=0)


def repack(ref, group, first, rows):
    main = dot(fine_of(2), chunk_rows(rows[:MAIN], 2)).astype(BF16)
    last = dot(fine_of(16), chunk_rows(rows[MAIN:], 16)).astype(BF16)
    put_tiles(ref, group, first, main)
    put_tiles(ref, group, first + TILES - 1, last)


def route_tables(routes_ref, weights_ref, experts):
    chosen, tokens = routes_ref.shape
    expert = iota((experts, tokens), 0)
    mask = jnp.zeros((experts, tokens), F32)
    weight = jnp.zeros((experts, tokens), F32)
    for k in range(chosen):
        hit = routes_ref[k : k + 1, :] == expert
        mask = mask + jnp.where(hit, 1.0, 0.0)
        weight = weight + jnp.where(hit, weights_ref[k : k + 1, :].astype(F32), 0.0)
    earlier = ones_where(iota((tokens, tokens), 0) < iota((tokens, tokens), 1))
    return jnp.where(mask > 0.5, dot(mask.astype(BF16), earlier), -1.0), weight


def pack_kernel(part, routes_ref, weights_ref, x_ref, dy_ref, send_ref, ranks_ref, rank_ref, weight_ref):
    step = pl.program_id(0)

    @pl.when(step == 0)
    def _():
        rank_ref[...], weight_ref[...] = route_tables(routes_ref, weights_ref, rank_ref.shape[0])

    here = pl.ds(pl.multiple_of(step * GROUP, GROUP), GROUP)
    ranks_ref[...] = rank_ref[here, :]
    ranks, weights = rank_ref[here, :], weight_ref[here, :]
    wide, weight = spread_rows(ranks), spread_rows(weights)
    fine = iota((FINE, LANES), 0) % 16
    main = wide == (part * SLOTS + fine // 2).astype(F32)
    over = ranks == float(PARTS * SLOTS + part)
    for first, ref, value, single in ((0, x_ref, 1.0, 1.0), (TILES, dy_ref, weight, weights)):
        rows = ref[...]
        pick = jnp.concatenate(
            [jnp.where(main & (fine % 2 == c), value, 0.0).astype(BF16) for c in range(2)], axis=1
        )
        put_tiles(send_ref, 0, first, dot(pick, chunk_rows(rows, 2)).astype(BF16))
        last = dot(jnp.where(over, single, 0.0).astype(BF16), rows).astype(BF16)
        piece = dot(fine_of(16), chunk_rows(last, 16))
        put_tiles(send_ref, 0, first + TILES - 1, piece.astype(BF16))


def expert_kernel(part, recv_ref, gate_ref, up_ref, down_ref, *refs):
    outs = refs[-6:-1] if part == 0 else refs[-5:]
    send_ref, x_ref, dy_ref, grads_ref, sh_ref = outs
    units = gate_ref.shape[1]
    x = jnp.concatenate([unpack(recv_ref, i, 0) for i in range(STEP)], axis=0)
    dy = jnp.concatenate([unpack(recv_ref, i, TILES) for i in range(STEP)], axis=0)
    x_ref[...] = x
    dy_ref[...] = dy
    pre_gate = dot(x, gate_ref[...])
    pre_up = dot(x, up_ref[...])
    back = dot_columns(dy, down_ref[...])
    sig = jax.nn.sigmoid(pre_gate)
    active = pre_gate * sig
    hidden = active * pre_up
    sh_ref[...] = hidden.astype(BF16)
    router = jnp.sum(back * hidden, axis=1, keepdims=True)
    gate_grads = (back * pre_up * sig * (1.0 + pre_gate * (1.0 - sig))).astype(BF16)
    up_grads = (back * active).astype(BF16)
    grads_ref[:, :units] = gate_grads
    grads_ref[:, units:] = up_grads
    token_part = dot_columns(gate_grads, gate_ref[...]) + dot_columns(up_grads, up_ref[...])
    token_part = token_part.astype(BF16)
    router = jnp.broadcast_to(router, (STEP * ROWS, LANES)).astype(BF16)
    if part == 0:
        refs[-1][...] = router
    for i in range(STEP):
        rows = slice(i * ROWS, (i + 1) * ROWS)
        repack(send_ref, i, 0, token_part[rows])
        if part == 1:
            both_parts = jnp.concatenate([refs[0][rows, :], router[rows]], axis=0)
            shape = (FINE, PARTS * ROWS)
            fine, col = iota(shape, 0), iota(shape, 1)
            s, q = fine // 16, fine % 16
            main = ones_where(col == (q // SLOTS) * ROWS + s * SLOTS + q % SLOTS)
            over = ones_where((q < PARTS) & (col == q * ROWS + MAIN + s))
            low = iota((FINE, LANES), 1) < LANES // 2
            tile = jnp.where(low, dot(main, both_parts), dot(over, both_parts))
            put_tiles(send_ref, i, TILES, tile.astype(BF16))


def add_rows(part, ref, ranks, total_ref):
    tokens = ranks.shape[1]
    across = ones_where(iota((GROUP, FINE), 0) == iota((GROUP, FINE), 1) // 16)
    by_token = dot_rows(ranks.astype(BF16), across)
    single = dot_rows(ranks.astype(BF16), unit(GROUP, GROUP))
    fine = iota((tokens, FINE), 1) % 16
    main = by_token == (part * SLOTS + fine // 2).astype(F32)
    tiles = get_tiles(ref, 0, 0, TILES - 1)
    half = [dot(ones_where(main & (fine % 2 == c)), tiles) for c in range(2)]
    last = dot(rows_of(16), get_tiles(ref, 0, TILES - 1, 1)).astype(BF16)
    over = ones_where(single == float(PARTS * SLOTS + part))
    total_ref[...] += jnp.concatenate(half, axis=1) + dot(over, chunk_columns(last, 16))


def first_sum_kernel(recv_ref, rank_ref, total_ref):
    @pl.when(pl.program_id(0) == 0)
    def _():
        total_ref[...] = jnp.zeros_like(total_ref)

    add_rows(0, recv_ref, rank_ref[...], total_ref)


def combine_kernel(
    recv_ref, rank_ref, first_ref, routes_ref, weights_ref, grad_ref, router_ref, total_ref, value_ref
):
    step = pl.program_id(0)
    chosen, tokens = routes_ref.shape

    @pl.when(step == 0)
    def _():
        total_ref[...] = first_ref[...]

    ranks = rank_ref[...]
    add_rows(1, recv_ref, ranks, total_ref)
    wide = spread_rows(ranks)
    place = iota((FINE, LANES), 0) % 16
    tile = get_tiles(recv_ref, 0, TILES, 1).astype(F32)
    middle = LANES // 2
    value = jnp.where(wide == place.astype(F32), tile[:, 0:1], 0.0) + jnp.where(
        wide == (PARTS * SLOTS + place).astype(F32), tile[:, middle : middle + 1], 0.0
    )
    here = pl.ds(pl.multiple_of(step * GROUP, GROUP), GROUP)
    value_ref[here, :] = jnp.sum(value.reshape(GROUP, 16, LANES), axis=1)

    @pl.when(step == pl.num_programs(0) - 1)
    def _():
        grad_ref[...] = total_ref[...].astype(BF16)
        expert = iota(value_ref.shape, 0)
        row = iota((chosen, tokens), 0)
        out = jnp.zeros((chosen, tokens), F32)
        for k in range(chosen):
            picked = jnp.where(routes_ref[k : k + 1, :] == expert, value_ref[...], 0.0)
            out = jnp.where(row == k, jnp.sum(picked, axis=0, keepdims=True), out)
        router_ref[...] = (out / weights_ref[...].astype(F32)).astype(BF16)


def whole(shape):
    return pl.BlockSpec(shape, lambda i: (0,) * len(shape), pipeline_mode=pl.Buffered(1))


def params(mib):
    return pltpu.CompilerParams(vmem_limit_bytes=mib * MIB, dimension_semantics=("arbitrary",))


def cost(flops, size):
    return pl.CostEstimate(flops=flops, bytes_accessed=size, transcendentals=0)


def by_group(size, high):
    return pl.BlockSpec((size, high, LANES), lambda i: (i, 0, 0))


def pack(part, experts, routes, weights, x, dy):
    tokens, width = x.shape
    high = 2 * TILES * 16
    return pl.pallas_call(
        functools.partial(pack_kernel, part),
        grid=(experts // GROUP,),
        in_specs=[whole(routes.shape), whole(weights.shape), whole(x.shape), whole(dy.shape)],
        out_specs=[by_group(GROUP, high), pl.BlockSpec((GROUP, tokens), lambda i: (i, 0))],
        out_shape=[
            jax.ShapeDtypeStruct((experts, high, LANES), BF16),
            jax.ShapeDtypeStruct((experts, tokens), F32),
        ],
        scratch_shapes=[pltpu.VMEM((experts, tokens), F32)] * 2,
        compiler_params=params(60),
        cost_estimate=cost(8 * experts * 16 * tokens * width, 2 * experts * high * LANES),
        name="pack_rows",
    )(routes, weights, x, dy)


def expert(part, recv, gate, up, down, held=()):
    sources = recv.shape[0]
    width, units = gate.shape
    rows = sources // GROUP * ROWS
    steps = sources // (STEP * GROUP)
    high = (TILES + part) * 16
    by_rows = lambda n: pl.BlockSpec((STEP * ROWS, n), lambda i: (i + part * steps, 0))
    router = pl.BlockSpec((STEP * ROWS, LANES), lambda i: (i, 0))
    anywhere = pl.BlockSpec(memory_space=pl.ANY)
    return pl.pallas_call(
        functools.partial(expert_kernel, part),
        grid=(steps,),
        in_specs=[by_group(STEP * GROUP, recv.shape[1])]
        + [whole(w.shape) for w in (gate, up, down)]
        + ([router] + [anywhere] * 4 if part else []),
        out_specs=[by_group(STEP * GROUP, high)]
        + [by_rows(n) for n in (width, width, 2 * units, units)]
        + ([] if part else [router]),
        out_shape=[jax.ShapeDtypeStruct((sources, high, LANES), BF16)]
        + [
            jax.ShapeDtypeStruct((PARTS * rows, n), BF16) for n in (width, width, 2 * units, units)
        ]
        + ([] if part else [jax.ShapeDtypeStruct((rows, LANES), BF16)]),
        input_output_aliases={5 + i: 1 + i for i in range(4)} if part else {},
        compiler_params=params(60),
        cost_estimate=cost(10 * rows * width * units, 30 * MIB),
        name="expert",
    )(recv, gate, up, down, *held)


def first_sum(recv, ranks, width):
    experts, tokens = ranks.shape
    return pl.pallas_call(
        first_sum_kernel,
        grid=(experts // GROUP,),
        in_specs=[
            by_group(GROUP, recv.shape[1]),
            pl.BlockSpec((GROUP, tokens), lambda i: (i, 0)),
        ],
        out_specs=pl.BlockSpec((tokens, width), lambda i: (0, 0)),
        out_shape=jax.ShapeDtypeStruct((tokens, width), F32),
        compiler_params=params(32),
        cost_estimate=cost(4 * experts * 9 * tokens * width, 4 * experts * 80 * LANES),
        name="first_sum",
    )(recv, ranks)


def combine(recv, ranks, first, routes, weights):
    experts = recv.shape[0]
    chosen, tokens = routes.shape
    width = first.shape[1]
    return pl.pallas_call(
        combine_kernel,
        grid=(experts // GROUP,),
        in_specs=[
            by_group(GROUP, recv.shape[1]),
            pl.BlockSpec((GROUP, tokens), lambda i: (i, 0)),
            whole(first.shape),
            whole(routes.shape),
            whole(weights.shape),
        ],
        out_specs=[
            pl.BlockSpec((tokens, width), lambda i: (0, 0)),
            pl.BlockSpec((chosen, tokens), lambda i: (0, 0)),
        ],
        out_shape=[
            jax.ShapeDtypeStruct((tokens, width), BF16),
            jax.ShapeDtypeStruct((chosen, tokens), BF16),
        ],
        scratch_shapes=[pltpu.VMEM((tokens, width), F32), pltpu.VMEM((experts, tokens), F32)],
        compiler_params=params(32),
        cost_estimate=cost(4 * experts * 9 * tokens * width, 4 * experts * 80 * LANES),
        name="combine_parts",
    )(recv, ranks, first, routes, weights)


def exchange(value):
    return lax.all_to_all(value, "expert", split_axis=0, concat_axis=0, tiled=True)


def half_kernel(half_ref, left_ref, right_ref, *refs):
    product = dot_rows(left_ref[...], right_ref[...])
    if len(refs) > 1 and refs[0].shape[1] == right_ref.shape[1]:
        product, refs = product + refs[0][...].astype(F32), refs[1:]
    width = right_ref.shape[1] // len(refs)
    for i, ref in enumerate(refs):
        ref[...] = product[:, i * width : (i + 1) * width].astype(BF16)


def half_product(half, left, right, tile, arrived=(), pieces=1):
    total, columns = left.shape
    width = right.shape[1]
    rows = columns // 2
    steps = rows // tile
    by_rows = lambda n: pl.BlockSpec((tile, n), lambda i, half: (i, 0))
    return pl.pallas_call(
        half_kernel,
        grid_spec=pltpu.PrefetchScalarGridSpec(
            num_scalar_prefetch=1,
            grid=(steps,),
            in_specs=[
                pl.BlockSpec((total, tile), lambda i, half: (0, half[0] * steps + i)),
                pl.BlockSpec(
                    right.shape, lambda i, half: (0, 0), pipeline_mode=pl.Buffered(1)
                ),
            ]
            + [by_rows(width) for _ in arrived],
            out_specs=[by_rows(width // pieces)] * pieces,
        ),
        out_shape=[jax.ShapeDtypeStruct((rows, width // pieces), BF16)] * pieces,
        compiler_params=params(60),
        cost_estimate=cost(2 * total * rows * width, 10 * MIB),
        name="half_product",
    )(half, left, right, *arrived)


def over_dp(value):
    return lax.ppermute(value, "dp", [(0, 1), (1, 0)])


def body(tokens, routes, router_weights, w_gate, w_up, w_down, out_grad):
    experts = lax.axis_size("expert")
    width = tokens.shape[1]
    gate, up, down = w_gate[0], w_up[0], w_down[0]
    routes, weights = routes.T, router_weights.T
    send, ranks = pack(0, experts, routes, weights, tokens, out_grad)
    recv = exchange(send)
    ranks, routes_b = lax.optimization_barrier((ranks, routes))
    send_2, _ = pack(1, experts, routes_b, weights, tokens, out_grad)
    recv_2 = exchange(send_2)
    send_back, *held, router = expert(0, recv, gate, up, down)
    recv_2, send_back = lax.optimization_barrier((recv_2, send_back))
    recv_back = exchange(send_back)
    send_back_2, x, dy, grads, hidden = expert(1, recv_2, gate, up, down, [router, *held])
    recv_back_2 = exchange(send_back_2)
    first = first_sum(recv_back, ranks, width)
    mine = lax.axis_index("dp").astype(jnp.int32).reshape(1)
    arrived = over_dp(half_product(1 - mine, x, grads, 256)[0])
    arrived_down = over_dp(half_product(1 - mine, hidden, dy, 128)[0])
    gate_grad, up_grad = half_product(mine, x, grads, 256, [arrived], 2)
    (down_grad,) = half_product(mine, hidden, dy, 128, [arrived_down])
    recv_back_2, gate_grad, up_grad, down_grad = lax.optimization_barrier(
        (recv_back_2, gate_grad, up_grad, down_grad)
    )
    tokens_grad, router_grad = combine(recv_back_2, ranks, first, routes, weights)
    return (tokens_grad, router_grad.T, gate_grad[None], up_grad[None], down_grad[None])


def solution(mesh):
    placed = (
        P(("dp", "expert"), None),
        P(("dp", "expert"), None),
        P(("dp", "expert"), None),
        P("expert", None, None),
        P("expert", None, None),
        P("expert", None, None),
        P(("dp", "expert"), None),
    )
    return jax.shard_map(
        body,
        mesh=mesh,
        in_specs=placed,
        out_specs=(
            P(("dp", "expert"), None),
            P(("dp", "expert"), None),
            P("expert", "dp", None),
            P("expert", "dp", None),
            P("expert", "dp", None),
        ),
        check_vma=False,
    )
```

time: 530 us -> 241 us (0.45)
  local copies, waits for them, and re-layouts: 119 us -> 5.32 us
  waiting for transfers between devices: 215 us -> 103 us
  Pallas kernels: 0 us -> 88.1 us
  matrix products: 63 us -> 0 us
  other arithmetic: 55 us -> 0 us
  starting transfers between devices: 54.9 us -> 39 us
  between operations: 14.5 us -> 0.72 us
    all_to_all x5 -> x4, waiting for transfers between devices: 215 us -> 99.5 us  [exchange(): lax.all_to_all(value, 'expert', split_axis=0, concat_axis=0, tiled=True)]
    pallas_call x0 -> x10, Pallas kernels: none -> 88.1 us  [the longest x2 39.4 us: expert(): pl.pallas_call(functools.partial(expert_kernel, part), grid=(steps,), in_...]
    dot_general x7 -> x0, matrix products: 63 us -> none  [the longest x2 24.9 us: contract_rows(): lax.dot_general(left, right, (((0,), (0,)), ((), ())), preferred_element_...]
    gather x6 -> x0, local copies, waits for them, and re-layouts: 49.5 us -> none  [the longest x1 11.8 us: body(): jnp.take(tokens, token_of, axis=0).reshape(experts, capacity, width)]
    reshape x9 -> x0, local copies, waits for them, and re-layouts: 46.7 us -> none  [the longest x1 8.15 us: body(): flat_dy = rows_dy.reshape(source_count * slot_count, row_width)]
    another operation x4 -> x0, other arithmetic: 35.9 us -> none
    all_to_all x5 -> x4, starting transfers between devices: 54.5 us -> 39 us  [exchange(): lax.all_to_all(value, 'expert', split_axis=0, concat_axis=0, tiled=True)]
    scatter x2 -> x0, local copies, waits for them, and re-layouts: 11.9 us -> none  [the longest x1 7.59 us: body(): filled = jnp.zeros((slot_total,), jnp.bfloat16).at[slot_of].set(1)]
  transfers between devices with their start and end apart: 7 -> 6, of which waited for: 3 -> 4; matrix products, arithmetic and copies ran while one was open for 29% -> 0% of each run, Pallas kernels for 0% -> 33%
where the time goes in v2:
time: 241 us; the launch traced here: 236 us
  waiting for transfers between devices  103 us (43%)
  Pallas kernels  88.1 us (37%)
  starting transfers between devices  39 us (16%)
  local copies, waits for them, and re-layouts  5.32 us (2%)
    all_to_all x4, waiting for transfers between devices, exchange(): lax.all_to_all(value, 'expert', split_axis=0, concat_axis=0, tiled=True)  99.5 us
    pallas_call x2, Pallas kernels, expert(): pl.pallas_call(functools.partial(expert_kernel, part), grid=(steps,), in_...  39.4 us
    all_to_all x4, starting transfers between devices, exchange(): lax.all_to_all(value, 'expert', split_axis=0, concat_axis=0, tiled=True)  39 us
    pallas_call x4, Pallas kernels, half_product(): pl.pallas_call(half_kernel, grid_spec=pltpu.PrefetchScalarGridSpec(num_sc...  29.3 us
    pallas_call x2, Pallas kernels, pack(): pl.pallas_call(functools.partial(pack_kernel, part), grid=(experts // GRO...  12.7 us
    unnamed x14, local copies, waits for them, and re-layouts  5.32 us
  transfers between devices with their start and end apart: 6, of which 4 were waited for; matrix products, arithmetic and copies ran while one was open for 0% of the time, Pallas kernels for 33%

profile of v2, /device:TPU:50, one launch (start us, length us, event | category | flops | bytes accessed | tf_op | source)
XLA Modules:
  0.0 236.4 jit_solution(3750101849093839185)
XLA Ops:
  0.6 6.3 %pack_rows.2 = (bf16[64,288,128]{2,1,0:T(8,128)(2,1)}, f32[64,128]{1,0:T(8,128)}) custom-call(s32[8,128]{1,0:T(8,128)} %bitcast.10, bf16[8,128]{1,0:T(8,128)(2,1)} %bitcast.13, bf16[128,2048]{1,0:T(8,128)(2,1)} %x_ref.3, bf16[128,2048]{1,0:T(8,128)(2,1)} %dy_ref.3), custom_call_target="tpu_custom_call" | custom-call | flops 2147483648 | bytes 4718592 | tf_op jit(solution)/shard_map/pack_rows/pallas_call | solution.py:262
  7.0 11.1 %all-to-all-start.1 = ((bf16[64,288,128]{2,1,0:T(8,128)(2,1)}), bf16[64,288,128]{2,1,0:T(8,128)(2,1)}, u32[]{:S(2)}, u32[]{:S(2)}) async-start(bf16[64,288,128]{2,1,0:T(8,128)(2,1)} %get-tuple-element.34), calls=%async_computation.1 | async-start | bytes 9437184 | tf_op jit(solution)/shard_map/all_to_all | solution.py:355
  18.1 6.4 %pack_rows.3 = (bf16[64,288,128]{2,1,0:T(8,128)(2,1)}, f32[64,128]{1,0:T(8,128)}) custom-call(s32[8,128]{1,0:T(8,128)} %bitcast.11, bf16[8,128]{1,0:T(8,128)(2,1)} %bitcast.14, bf16[128,2048]{1,0:T(8,128)(2,1)} %x_ref.3, bf16[128,2048]{1,0:T(8,128)(2,1)} %dy_ref.3), custom_call_target="tpu_custom_call" | custom-call | flops 2147483648 | bytes 4718592 | tf_op jit(solution)/shard_map/pack_rows/pallas_call | solution.py:262
  24.4 55.0 %all-to-all-done.1.recv_ref = bf16[64,288,128]{2,1,0:T(8,128)(2,1)} async-done(((bf16[64,288,128]{2,1,0:T(8,128)(2,1)}), bf16[64,288,128]{2,1,0:T(8,128)(2,1)}, u32[]{:S(2)}, u32[]{:S(2)}) %all-to-all-start.1) | async-done | bytes 4718624 | tf_op jit(solution)/shard_map/all_to_all | solution.py:355
  79.5 8.3 %all-to-all-start = ((bf16[64,288,128]{2,1,0:T(8,128)(2,1)}), bf16[64,288,128]{2,1,0:T(8,128)(2,1)}, u32[]{:S(2)}, u32[]{:S(2)}) async-start(bf16[64,288,128]{2,1,0:T(8,128)(2,1)} %get-tuple-element.33), calls=%async_computation | async-start | bytes 9437184 | tf_op jit(solution)/shard_map/all_to_all | solution.py:355
  87.8 19.0 %expert.2 = (bf16[64,144,128]{2,1,0:T(8,128)(2,1)}, bf16[1152,2048]{1,0:T(8,128)(2,1)}, bf16[1152,2048]{1,0:T(8,128)(2,1)}, bf16[1152,1536]{1,0:T(8,128)(2,1)}, ...) custom-call(bf16[64,288,128]{2,1,0:T(8,128)(2,1)} %all-to-all-done.1.recv_ref, bf16[2048,768]{1,0:T(8,128)(2,1)} %bitcast.17, ...), custom_call_target="tpu_custom_call" | custom-call | flops 9059696640 | bytes 31457280 | tf_op jit(solution)/shard_map/expert/pallas_call | solution.py:287
  106.8 42.3 %all-to-all-done.recv_ref = bf16[64,288,128]{2,1,0:T(8,128)(2,1)} async-done(((bf16[64,288,128]{2,1,0:T(8,128)(2,1)}), bf16[64,288,128]{2,1,0:T(8,128)(2,1)}, u32[]{:S(2)}, u32[]{:S(2)}) %all-to-all-start) | async-done | bytes 4718624 | tf_op jit(solution)/shard_map/all_to_all | solution.py:355
  149.1 9.2 %all-to-all-start.3 = ((bf16[64,144,128]{2,1,0:T(8,128)(2,1)}), bf16[64,144,128]{2,1,0:T(8,128)(2,1)S(1)}, u32[]{:S(2)}, u32[]{:S(2)}) async-start(bf16[64,144,128]{2,1,0:T(8,128)(2,1)} %get-tuple-element.51), calls=%async_computation.3 | async-start | bytes 4718592 | tf_op jit(solution)/shard_map/all_to_all | solution.py:355
  158.3 20.4 %expert.3 = (bf16[64,160,128]{2,1,0:T(8,128)(2,1)}, bf16[1152,2048]{1,0:T(8,128)(2,1)}, bf16[1152,2048]{1,0:T(8,128)(2,1)}, bf16[1152,1536]{1,0:T(8,128)(2,1)}, bf16[1152,768]{1,0:T(8,128)(2,1)}) custom-call(bf16[64,288,128]{2,1,0:T(8,128)(2,1)} %all-to-all-done.recv_ref, ...), custom_call_target="tpu_custom_call", output_to_operand_aliasing={{1}: (5, {}), {2}: (6, {}), {3}: (7, {}), {4}: (8, {})} | custom-call | flops 9059696640 | bytes 31457280 | tf_op jit(solution)/shard_map/expert/pallas_call | solution.py:287
  178.7 8.2 %half_product.4 = bf16[1024,1536]{1,0:T(8,128)(2,1)} custom-call(s32[1]{0:T(128)S(6)} %sub.4.half_ref, bf16[1152,2048]{1,0:T(8,128)(2,1)} %get-tuple-element.43.left_ref, bf16[1152,1536]{1,0:T(8,128)(2,1)} %get-tuple-element.44.right_ref), custom_call_target="tpu_custom_call" | custom-call | flops 3623878656 | bytes 10485760 | tf_op jit(solution)/shard_map/half_product/pallas_call | solution.py:373
  186.9 0.0 collective-permute-start
  186.9 0.0 all-to-all-done.3.recv_ref
  186.9 0.0 copy-start
  186.9 1.4 copy-done
  188.4 10.3 %all-to-all-start.2 = ((bf16[64,160,128]{2,1,0:T(8,128)(2,1)}), bf16[64,160,128]{2,1,0:T(8,128)(2,1)S(1)}, u32[]{:S(2)}, u32[]{:S(2)}) async-start(bf16[64,160,128]{2,1,0:T(8,128)(2,1)} %get-tuple-element.42), calls=%async_computation.2 | async-start | bytes 5242880 | tf_op jit(solution)/shard_map/all_to_all | solution.py:355
  198.7 6.2 %half_product.6 = bf16[384,2048]{1,0:T(8,128)(2,1)} custom-call(s32[1]{0:T(128)S(6)} %sub.4.half_ref, bf16[1152,768]{1,0:T(8,128)(2,1)} %get-tuple-element.47.left_ref, bf16[1152,2048]{1,0:T(8,128)(2,1)} %get-tuple-element.48.right_ref), custom_call_target="tpu_custom_call" | custom-call | flops 1811939328 | bytes 10485760 | tf_op jit(solution)/shard_map/half_product/pallas_call | solution.py:373
  204.9 0.0 copy-start.4
  204.9 0.0 collective-permute-start.1
  204.9 3.7 %collective-permute-done.1.refs_0_ = bf16[384,2048]{1,0:T(8,128)(2,1)} collective-permute-done((bf16[384,2048]{1,0:T(8,128)(2,1)}, bf16[384,2048]{1,0:T(8,128)(2,1)}, u32[]{:S(2)}, u32[]{:S(2)}) %collective-permute-start.1) | collective-permute-done | bytes 1572896 | tf_op jit(solution)/shard_map/ppermute | solution.py:395
  208.6 6.5 %half_product.7 = bf16[384,2048]{1,0:T(8,128)(2,1)} custom-call(s32[1]{0:T(128)} %bitcast.5.half_ref, bf16[1152,768]{1,0:T(8,128)(2,1)} %get-tuple-element.47.left_ref, bf16[1152,2048]{1,0:T(8,128)(2,1)} %get-tuple-element.48.right_ref, bf16[384,2048]{1,0:T(8,128)(2,1)} %collective-permute-done.1.refs_0_), custom_call_target="tpu_custom_call" | custom-call | flops 1811939328 | bytes 10485760 | tf_op jit(solution)/shard_map/half_product/pallas_call | solution.py:373
  215.2 0.0 copy-done.4
  215.2 0.0 copy-start.1
  215.2 1.7 copy-done.1
  216.8 2.9 %first_sum.1.first_ref = f32[128,2048]{1,0:T(8,128)S(1)} custom-call(bf16[64,144,128]{2,1,0:T(8,128)(2,1)S(1)} %copy-done.1, f32[64,128]{1,0:T(8,128)S(1)} %copy-done.4), custom_call_target="tpu_custom_call" | custom-call | flops 603979776 | bytes 2621440 | tf_op jit(solution)/shard_map/first_sum/pallas_call | solution.py:310
  219.8 0.0 copy-start.2
  219.8 1.0 copy-done.2
  220.7 0.0 copy-start.5
  220.7 0.0 copy-start.6
  220.7 0.0 collective-permute-done.refs_0_
  220.8 8.4 %half_product.5 = (bf16[1024,768]{1,0:T(8,128)(2,1)}, bf16[1024,768]{1,0:T(8,128)(2,1)}) custom-call(s32[1]{0:T(128)} %bitcast.5.half_ref, bf16[1152,2048]{1,0:T(8,128)(2,1)} %get-tuple-element.43.left_ref, bf16[1152,1536]{1,0:T(8,128)(2,1)} %get-tuple-element.44.right_ref, bf16[1024,1536]{1,0:T(8,128)(2,1)} %collective-permute-done.refs_0_), custom_call_target="tpu_custom_call" | custom-call | flops 3623878656 | bytes 10485760 | tf_op jit(solution)/shard_map/half_product/pallas_call | solution.py:373
  229.2 2.2 all-to-all-done.2.recv_ref
  231.4 0.0 copy-done.5
  231.4 0.0 copy-done.6
  231.4 0.0 copy-start.3
  231.4 1.2 copy-done.3
  232.6 3.8 %combine_parts.1 = (bf16[128,2048]{1,0:T(8,128)(2,1)}, bf16[8,128]{1,0:T(8,128)(2,1)}) custom-call(bf16[64,160,128]{2,1,0:T(8,128)(2,1)S(1)} %all-to-all-done.2.recv_ref, f32[64,128]{1,0:T(8,128)S(1)} %copy-done.4, f32[128,2048]{1,0:T(8,128)S(1)} %copy-done.3, s32[8,128]{1,0:T(8,128)S(1)} %bitcast.12, bf16[8,128]{1,0:T(8,128)(2,1)S(1)} %bitcast.15), custom_call_target="tpu_custom_call" | custom-call | flops 603979776 | bytes 2621440 | tf_op jit(solution)/shard_map/combine_parts/pallas_call | solution.py:329
Async XLA Ops:
  7.0 72.5 %all-to-all-start.1 = ((bf16[64,288,128]{2,1,0:T(8,128)(2,1)}), bf16[64,288,128]{2,1,0:T(8,128)(2,1)}, u32[]{:S(2)}, u32[]{:S(2)}) async-start(bf16[64,288,128]{2,1,0:T(8,128)(2,1)} %get-tuple-element.34), calls=%async_computation.1 | async-start | bytes 9437184 | tf_op jit(solution)/shard_map/all_to_all | solution.py:355
  79.5 69.6 %all-to-all-start = ((bf16[64,288,128]{2,1,0:T(8,128)(2,1)}), bf16[64,288,128]{2,1,0:T(8,128)(2,1)}, u32[]{:S(2)}, u32[]{:S(2)}) async-start(bf16[64,288,128]{2,1,0:T(8,128)(2,1)} %get-tuple-element.33), calls=%async_computation | async-start | bytes 9437184 | tf_op jit(solution)/shard_map/all_to_all | solution.py:355
  149.1 37.8 %all-to-all-start.3 = ((bf16[64,144,128]{2,1,0:T(8,128)(2,1)}), bf16[64,144,128]{2,1,0:T(8,128)(2,1)S(1)}, u32[]{:S(2)}, u32[]{:S(2)}) async-start(bf16[64,144,128]{2,1,0:T(8,128)(2,1)} %get-tuple-element.51), calls=%async_computation.3 | async-start | bytes 4718592 | tf_op jit(solution)/shard_map/all_to_all | solution.py:355
  186.9 33.9 %collective-permute-start = (bf16[1024,1536]{1,0:T(8,128)(2,1)}, bf16[1024,1536]{1,0:T(8,128)(2,1)}, u32[]{:S(2)}, u32[]{:S(2)}) collective-permute-start(bf16[1024,1536]{1,0:T(8,128)(2,1)} %half_product.4), channel_id=1, source_target_pairs={{0,64},{64,0},{1,65},{65,1},{2,66},{66,2},{3,67},{67,3},{4,68},{68... | collective-permute-start | bytes 9437192 | tf_op jit(solution)/shard_map/ppermute | solution.py:395
  186.9 1.5 copy-start
  188.4 43.0 %all-to-all-start.2 = ((bf16[64,160,128]{2,1,0:T(8,128)(2,1)}), bf16[64,160,128]{2,1,0:T(8,128)(2,1)S(1)}, u32[]{:S(2)}, u32[]{:S(2)}) async-start(bf16[64,160,128]{2,1,0:T(8,128)(2,1)} %get-tuple-element.42), calls=%async_computation.2 | async-start | bytes 5242880 | tf_op jit(solution)/shard_map/all_to_all | solution.py:355
  204.9 10.3 %copy-start.4 = (f32[64,128]{1,0:T(8,128)S(1)}, f32[64,128]{1,0:T(8,128)}, u32[]{:S(2)}) copy-start(f32[64,128]{1,0:T(8,128)} %get-tuple-element.50.rank_ref) | copy-start | bytes 98308
  204.9 3.8 %collective-permute-start.1 = (bf16[384,2048]{1,0:T(8,128)(2,1)}, bf16[384,2048]{1,0:T(8,128)(2,1)}, u32[]{:S(2)}, u32[]{:S(2)}) collective-permute-start(bf16[384,2048]{1,0:T(8,128)(2,1)} %half_product.6), channel_id=1, source_target_pairs={{0,64},{64,0},{1,65},{65,1},{2,66},{66,2},{3,67},{67,3},{4,68},{68... | collective-permute-start | bytes 4718600 | tf_op jit(solution)/shard_map/ppermute | solution.py:395
  215.2 1.7 copy-start.1
  219.8 1.0 copy-start.2
  220.7 10.6 %copy-start.5 = (s32[128,8]{0,1:T(8,128)S(1)}, s32[128,8]{0,1:T(8,128)}, u32[]{:S(2)}) copy-start(s32[128,8]{0,1:T(8,128)} %param.8) | copy-start | bytes 12292
  220.7 10.6 %copy-start.6 = (bf16[128,8]{0,1:T(8,128)(2,1)S(1)}, bf16[128,8]{0,1:T(8,128)(2,1)}, u32[]{:S(2)}) copy-start(bf16[128,8]{0,1:T(8,128)(2,1)} %param.9) | copy-start | bytes 6148
  231.4 1.2 copy-start.3

commit v3 on v2

--- a/solution.py
+++ b/solution.py
@@ -316,7 +316,7 @@
         ],
         out_specs=pl.BlockSpec((tokens, width), lambda i: (0, 0)),
         out_shape=jax.ShapeDtypeStruct((tokens, width), F32),
-        compiler_params=params(32),
+        compiler_params=params(60),
         cost_estimate=cost(4 * experts * 9 * tokens * width, 4 * experts * 80 * LANES),
         name="first_sum",
     )(recv, ranks)
@@ -345,7 +345,7 @@
             jax.ShapeDtypeStruct((chosen, tokens), BF16),
         ],
         scratch_shapes=[pltpu.VMEM((tokens, width), F32), pltpu.VMEM((experts, tokens), F32)],
-        compiler_params=params(32),
+        compiler_params=params(60),
         cost_estimate=cost(4 * experts * 9 * tokens * width, 4 * experts * 80 * LANES),
         name="combine_parts",
     )(recv, ranks, first, routes, weights)

time: 241 us -> 243 us (level)
  Pallas kernels: 88.1 us -> 92.4 us
    pallas_call x1, Pallas kernels: 2.93 us -> 5.39 us  [first_sum(): pl.pallas_call(first_sum_kernel, grid=(experts // GROUP,), in_specs=[by_g...]
    unnamed x14 -> x4, local copies, waits for them, and re-layouts: 5.32 us -> 2.96 us
  transfers between devices with their start and end apart: 6 -> 6, of which waited for: 4 -> 4; matrix products, arithmetic and copies ran while one was open for 0% -> 0% of each run, Pallas kernels for 33% -> 34%
where the time goes in v3:
time: 243 us; the launch traced here: 239 us
  waiting for transfers between devices  103 us (42%)
  Pallas kernels  92.4 us (38%)
  starting transfers between devices  39.1 us (16%)
  local copies, waits for them, and re-layouts  2.96 us (1%)
    all_to_all x4, waiting for transfers between devices, exchange(): lax.all_to_all(value, 'expert', split_axis=0, concat_axis=0, tiled=True)  99.7 us
    pallas_call x2, Pallas kernels, expert(): pl.pallas_call(functools.partial(expert_kernel, part), grid=(steps,), in_...  39.3 us
    all_to_all x4, starting transfers between devices, exchange(): lax.all_to_all(value, 'expert', split_axis=0, concat_axis=0, tiled=True)  39.1 us
    pallas_call x4, Pallas kernels, half_product(): pl.pallas_call(half_kernel, grid_spec=pltpu.PrefetchScalarGridSpec(num_sc...  29.3 us
    pallas_call x2, Pallas kernels, pack(): pl.pallas_call(functools.partial(pack_kernel, part), grid=(experts // GRO...  12.7 us
    pallas_call x1, Pallas kernels, combine(): pl.pallas_call(combine_kernel, grid=(experts // GROUP,), in_specs=[by_gro...  5.75 us
    pallas_call x1, Pallas kernels, first_sum(): pl.pallas_call(first_sum_kernel, grid=(experts // GROUP,), in_specs=[by_g...  5.39 us
  transfers between devices with their start and end apart: 6, of which 4 were waited for; matrix products, arithmetic and copies ran while one was open for 0% of the time, Pallas kernels for 34%

profile of v3, /device:TPU:50, one launch (start us, length us, event | category | flops | bytes accessed | tf_op | source)
XLA Modules:
  0.0 238.5 jit_solution(6246164141750819803)
XLA Ops:
  0.6 6.3 %pack_rows.2 = (bf16[64,288,128]{2,1,0:T(8,128)(2,1)}, f32[64,128]{1,0:T(8,128)}) custom-call(s32[8,128]{1,0:T(8,128)} %bitcast.11, bf16[8,128]{1,0:T(8,128)(2,1)} %bitcast.14, bf16[128,2048]{1,0:T(8,128)(2,1)} %x_ref.3, bf16[128,2048]{1,0:T(8,128)(2,1)} %dy_ref.3), custom_call_target="tpu_custom_call" | custom-call | flops 2147483648 | bytes 4718592 | tf_op jit(solution)/shard_map/pack_rows/pallas_call | solution.py:262
  7.0 11.1 %all-to-all-start.1 = ((bf16[64,288,128]{2,1,0:T(8,128)(2,1)}), bf16[64,288,128]{2,1,0:T(8,128)(2,1)}, u32[]{:S(2)}, u32[]{:S(2)}) async-start(bf16[64,288,128]{2,1,0:T(8,128)(2,1)} %get-tuple-element.34), calls=%async_computation.1 | async-start | bytes 9437184 | tf_op jit(solution)/shard_map/all_to_all | solution.py:355
  18.1 6.3 %pack_rows.3 = (bf16[64,288,128]{2,1,0:T(8,128)(2,1)}, f32[64,128]{1,0:T(8,128)}) custom-call(s32[8,128]{1,0:T(8,128)} %bitcast.12, bf16[8,128]{1,0:T(8,128)(2,1)} %bitcast.15, bf16[128,2048]{1,0:T(8,128)(2,1)} %x_ref.3, bf16[128,2048]{1,0:T(8,128)(2,1)} %dy_ref.3), custom_call_target="tpu_custom_call" | custom-call | flops 2147483648 | bytes 4718592 | tf_op jit(solution)/shard_map/pack_rows/pallas_call | solution.py:262
  24.4 55.0 %all-to-all-done.1.recv_ref = bf16[64,288,128]{2,1,0:T(8,128)(2,1)} async-done(((bf16[64,288,128]{2,1,0:T(8,128)(2,1)}), bf16[64,288,128]{2,1,0:T(8,128)(2,1)}, u32[]{:S(2)}, u32[]{:S(2)}) %all-to-all-start.1) | async-done | bytes 4718624 | tf_op jit(solution)/shard_map/all_to_all | solution.py:355
  79.4 8.4 %all-to-all-start = ((bf16[64,288,128]{2,1,0:T(8,128)(2,1)}), bf16[64,288,128]{2,1,0:T(8,128)(2,1)}, u32[]{:S(2)}, u32[]{:S(2)}) async-start(bf16[64,288,128]{2,1,0:T(8,128)(2,1)} %get-tuple-element.33), calls=%async_computation | async-start | bytes 9437184 | tf_op jit(solution)/shard_map/all_to_all | solution.py:355
  87.8 19.0 %expert.2 = (bf16[64,144,128]{2,1,0:T(8,128)(2,1)}, bf16[1152,2048]{1,0:T(8,128)(2,1)}, bf16[1152,2048]{1,0:T(8,128)(2,1)}, bf16[1152,1536]{1,0:T(8,128)(2,1)}, ...) custom-call(bf16[64,288,128]{2,1,0:T(8,128)(2,1)} %all-to-all-done.1.recv_ref, bf16[2048,768]{1,0:T(8,128)(2,1)} %bitcast.17, ...), custom_call_target="tpu_custom_call" | custom-call | flops 9059696640 | bytes 31457280 | tf_op jit(solution)/shard_map/expert/pallas_call | solution.py:287
  106.8 42.3 %all-to-all-done.recv_ref = bf16[64,288,128]{2,1,0:T(8,128)(2,1)} async-done(((bf16[64,288,128]{2,1,0:T(8,128)(2,1)}), bf16[64,288,128]{2,1,0:T(8,128)(2,1)}, u32[]{:S(2)}, u32[]{:S(2)}) %all-to-all-start) | async-done | bytes 4718624 | tf_op jit(solution)/shard_map/all_to_all | solution.py:355
  149.0 9.2 %all-to-all-start.3 = ((bf16[64,144,128]{2,1,0:T(8,128)(2,1)}), bf16[64,144,128]{2,1,0:T(8,128)(2,1)S(1)}, u32[]{:S(2)}, u32[]{:S(2)}) async-start(bf16[64,144,128]{2,1,0:T(8,128)(2,1)} %get-tuple-element.51), calls=%async_computation.3 | async-start | bytes 4718592 | tf_op jit(solution)/shard_map/all_to_all | solution.py:355
  158.3 20.3 %expert.3 = (bf16[64,160,128]{2,1,0:T(8,128)(2,1)}, bf16[1152,2048]{1,0:T(8,128)(2,1)}, bf16[1152,2048]{1,0:T(8,128)(2,1)}, bf16[1152,1536]{1,0:T(8,128)(2,1)}, bf16[1152,768]{1,0:T(8,128)(2,1)}) custom-call(bf16[64,288,128]{2,1,0:T(8,128)(2,1)} %all-to-all-done.recv_ref, ...), custom_call_target="tpu_custom_call", output_to_operand_aliasing={{1}: (5, {}), {2}: (6, {}), {3}: (7, {}), {4}: (8, {})} | custom-call | flops 9059696640 | bytes 31457280 | tf_op jit(solution)/shard_map/expert/pallas_call | solution.py:287
  178.6 8.2 %half_product.4 = bf16[1024,1536]{1,0:T(8,128)(2,1)} custom-call(s32[1]{0:T(128)S(6)} %sub.4.half_ref, bf16[1152,2048]{1,0:T(8,128)(2,1)} %get-tuple-element.43.left_ref, bf16[1152,1536]{1,0:T(8,128)(2,1)} %get-tuple-element.44.right_ref), custom_call_target="tpu_custom_call" | custom-call | flops 3623878656 | bytes 10485760 | tf_op jit(solution)/shard_map/half_product/pallas_call | solution.py:373
  186.8 0.0 collective-permute-start
  186.8 0.0 all-to-all-done.3.recv_ref
  186.8 0.0 copy-start.1
  186.8 1.5 copy-done.1
  188.2 10.3 %all-to-all-start.2 = ((bf16[64,160,128]{2,1,0:T(8,128)(2,1)}), bf16[64,160,128]{2,1,0:T(8,128)(2,1)S(1)}, u32[]{:S(2)}, u32[]{:S(2)}) async-start(bf16[64,160,128]{2,1,0:T(8,128)(2,1)} %get-tuple-element.42), calls=%async_computation.2 | async-start | bytes 5242880 | tf_op jit(solution)/shard_map/all_to_all | solution.py:355
  198.6 6.2 %half_product.6 = bf16[384,2048]{1,0:T(8,128)(2,1)} custom-call(s32[1]{0:T(128)S(6)} %sub.4.half_ref, bf16[1152,768]{1,0:T(8,128)(2,1)} %get-tuple-element.47.left_ref, bf16[1152,2048]{1,0:T(8,128)(2,1)} %get-tuple-element.48.right_ref), custom_call_target="tpu_custom_call" | custom-call | flops 1811939328 | bytes 10485760 | tf_op jit(solution)/shard_map/half_product/pallas_call | solution.py:373
  204.8 0.0 collective-permute-start.1
  204.8 3.7 %collective-permute-done.1.refs_0_ = bf16[384,2048]{1,0:T(8,128)(2,1)} collective-permute-done((bf16[384,2048]{1,0:T(8,128)(2,1)}, bf16[384,2048]{1,0:T(8,128)(2,1)}, u32[]{:S(2)}, u32[]{:S(2)}) %collective-permute-start.1) | collective-permute-done | bytes 1572896 | tf_op jit(solution)/shard_map/ppermute | solution.py:395
  208.5 6.5 %half_product.7 = bf16[384,2048]{1,0:T(8,128)(2,1)} custom-call(s32[1]{0:T(128)} %bitcast.5.half_ref, bf16[1152,768]{1,0:T(8,128)(2,1)} %get-tuple-element.47.left_ref, bf16[1152,2048]{1,0:T(8,128)(2,1)} %get-tuple-element.48.right_ref, bf16[384,2048]{1,0:T(8,128)(2,1)} %collective-permute-done.1.refs_0_), custom_call_target="tpu_custom_call" | custom-call | flops 1811939328 | bytes 10485760 | tf_op jit(solution)/shard_map/half_product/pallas_call | solution.py:373
  215.1 5.4 %first_sum.1.first_ref = f32[128,2048]{1,0:T(8,128)} custom-call(bf16[64,144,128]{2,1,0:T(8,128)(2,1)} %copy-done.1, f32[64,128]{1,0:T(8,128)} %get-tuple-element.50.rank_ref), custom_call_target="tpu_custom_call" | custom-call | flops 603979776 | bytes 2621440 | tf_op jit(solution)/shard_map/first_sum/pallas_call | solution.py:310
  220.5 0.0 collective-permute-done.refs_0_
  220.5 8.4 %half_product.5 = (bf16[1024,768]{1,0:T(8,128)(2,1)}, bf16[1024,768]{1,0:T(8,128)(2,1)}) custom-call(s32[1]{0:T(128)} %bitcast.5.half_ref, bf16[1152,2048]{1,0:T(8,128)(2,1)} %get-tuple-element.43.left_ref, bf16[1152,1536]{1,0:T(8,128)(2,1)} %get-tuple-element.44.right_ref, bf16[1024,1536]{1,0:T(8,128)(2,1)} %collective-permute-done.refs_0_), custom_call_target="tpu_custom_call" | custom-call | flops 3623878656 | bytes 10485760 | tf_op jit(solution)/shard_map/half_product/pallas_call | solution.py:373
  228.8 2.4 %all-to-all-done.2.recv_ref = bf16[64,160,128]{2,1,0:T(8,128)(2,1)S(1)} async-done(((bf16[64,160,128]{2,1,0:T(8,128)(2,1)}), bf16[64,160,128]{2,1,0:T(8,128)(2,1)S(1)}, u32[]{:S(2)}, u32[]{:S(2)}) %all-to-all-start.2) | async-done | bytes 2621472 | tf_op jit(solution)/shard_map/all_to_all | solution.py:355
  231.3 0.0 copy-start
  231.3 1.5 copy-done
  232.8 5.7 %combine_parts.1 = (bf16[128,2048]{1,0:T(8,128)(2,1)}, bf16[8,128]{1,0:T(8,128)(2,1)}) custom-call(bf16[64,160,128]{2,1,0:T(8,128)(2,1)} %copy-done, f32[64,128]{1,0:T(8,128)} %get-tuple-element.50.rank_ref, f32[128,2048]{1,0:T(8,128)} %first_sum.1.first_ref, s32[8,128]{1,0:T(8,128)} %bitcast.13, bf16[8,128]{1,0:T(8,128)(2,1)} %bitcast.16), custom_call_target="tpu_custom_call" | custom-call | flops 603979776 | bytes 2621440 | tf_op jit(solution)/shard_map/combine_parts/pallas_call | solution.py:329
Async XLA Ops:
  7.0 72.4 %all-to-all-start.1 = ((bf16[64,288,128]{2,1,0:T(8,128)(2,1)}), bf16[64,288,128]{2,1,0:T(8,128)(2,1)}, u32[]{:S(2)}, u32[]{:S(2)}) async-start(bf16[64,288,128]{2,1,0:T(8,128)(2,1)} %get-tuple-element.34), calls=%async_computation.1 | async-start | bytes 9437184 | tf_op jit(solution)/shard_map/all_to_all | solution.py:355
  79.4 69.7 %all-to-all-start = ((bf16[64,288,128]{2,1,0:T(8,128)(2,1)}), bf16[64,288,128]{2,1,0:T(8,128)(2,1)}, u32[]{:S(2)}, u32[]{:S(2)}) async-start(bf16[64,288,128]{2,1,0:T(8,128)(2,1)} %get-tuple-element.33), calls=%async_computation | async-start | bytes 9437184 | tf_op jit(solution)/shard_map/all_to_all | solution.py:355
  149.0 37.7 %all-to-all-start.3 = ((bf16[64,144,128]{2,1,0:T(8,128)(2,1)}), bf16[64,144,128]{2,1,0:T(8,128)(2,1)S(1)}, u32[]{:S(2)}, u32[]{:S(2)}) async-start(bf16[64,144,128]{2,1,0:T(8,128)(2,1)} %get-tuple-element.51), calls=%async_computation.3 | async-start | bytes 4718592 | tf_op jit(solution)/shard_map/all_to_all | solution.py:355
  186.8 33.7 %collective-permute-start = (bf16[1024,1536]{1,0:T(8,128)(2,1)}, bf16[1024,1536]{1,0:T(8,128)(2,1)}, u32[]{:S(2)}, u32[]{:S(2)}) collective-permute-start(bf16[1024,1536]{1,0:T(8,128)(2,1)} %half_product.4), channel_id=1, source_target_pairs={{0,64},{64,0},{1,65},{65,1},{2,66},{66,2},{3,67},{67,3},{4,68},{68... | collective-permute-start | bytes 9437192 | tf_op jit(solution)/shard_map/ppermute | solution.py:395
  186.8 1.5 copy-start.1
  188.2 43.0 %all-to-all-start.2 = ((bf16[64,160,128]{2,1,0:T(8,128)(2,1)}), bf16[64,160,128]{2,1,0:T(8,128)(2,1)S(1)}, u32[]{:S(2)}, u32[]{:S(2)}) async-start(bf16[64,160,128]{2,1,0:T(8,128)(2,1)} %get-tuple-element.42), calls=%async_computation.2 | async-start | bytes 5242880 | tf_op jit(solution)/shard_map/all_to_all | solution.py:355
  204.8 3.8 %collective-permute-start.1 = (bf16[384,2048]{1,0:T(8,128)(2,1)}, bf16[384,2048]{1,0:T(8,128)(2,1)}, u32[]{:S(2)}, u32[]{:S(2)}) collective-permute-start(bf16[384,2048]{1,0:T(8,128)(2,1)} %half_product.6), channel_id=1, source_target_pairs={{0,64},{64,0},{1,65},{65,1},{2,66},{66,2},{3,67},{67,3},{4,68},{68... | collective-permute-start | bytes 4718600 | tf_op jit(solution)/shard_map/ppermute | solution.py:395
  231.3 1.5 copy-start

commit v4 on v2

--- a/solution.py
+++ b/solution.py
@@ -207,14 +207,26 @@
 
 
 def combine_kernel(
-    recv_ref, rank_ref, first_ref, routes_ref, weights_ref, grad_ref, router_ref, total_ref, value_ref
+    recv_ref,
+    rank_ref,
+    first_hbm,
+    routes_ref,
+    weights_ref,
+    grad_ref,
+    router_ref,
+    total_ref,
+    value_ref,
+    first_ref,
+    copied,
 ):
     step = pl.program_id(0)
+    copy = pltpu.make_async_copy(first_hbm, first_ref, copied)
     chosen, tokens = routes_ref.shape
 
     @pl.when(step == 0)
     def _():
-        total_ref[...] = first_ref[...]
+        copy.start()
+        total_ref[...] = jnp.zeros_like(total_ref)
 
     ranks = rank_ref[...]
     add_rows(1, recv_ref, ranks, total_ref)
@@ -230,7 +242,8 @@
 
     @pl.when(step == pl.num_programs(0) - 1)
     def _():
-        grad_ref[...] = total_ref[...].astype(BF16)
+        copy.wait()
+        grad_ref[...] = (total_ref[...] + first_ref[...]).astype(BF16)
         expert = iota(value_ref.shape, 0)
         row = iota((chosen, tokens), 0)
         out = jnp.zeros((chosen, tokens), F32)
@@ -332,7 +345,7 @@
         in_specs=[
             by_group(GROUP, recv.shape[1]),
             pl.BlockSpec((GROUP, tokens), lambda i: (i, 0)),
-            whole(first.shape),
+            pl.BlockSpec(memory_space=pltpu.HBM),
             whole(routes.shape),
             whole(weights.shape),
         ],
@@ -344,7 +357,12 @@
             jax.ShapeDtypeStruct((tokens, width), BF16),
             jax.ShapeDtypeStruct((chosen, tokens), BF16),
         ],
-        scratch_shapes=[pltpu.VMEM((tokens, width), F32), pltpu.VMEM((experts, tokens), F32)],
+        scratch_shapes=[
+            pltpu.VMEM((tokens, width), F32),
+            pltpu.VMEM((experts, tokens), F32),
+            pltpu.VMEM((tokens, width), F32),
+            pltpu.SemaphoreType.DMA,
+        ],
         compiler_params=params(32),
         cost_estimate=cost(4 * experts * 9 * tokens * width, 4 * experts * 80 * LANES),
         name="combine_parts",

time: 241 us -> 241 us (level)
  no operation moved by 1% of the time
where the time goes in v4:
time: 241 us; the launch traced here: 237 us
  waiting for transfers between devices  103 us (43%)
  Pallas kernels  88.3 us (37%)
  starting transfers between devices  39 us (16%)
  local copies, waits for them, and re-layouts  5.32 us (2%)
    all_to_all x4, waiting for transfers between devices, exchange(): lax.all_to_all(value, 'expert', split_axis=0, concat_axis=0, tiled=True)  99.5 us
    pallas_call x2, Pallas kernels, expert(): pl.pallas_call(functools.partial(expert_kernel, part), grid=(steps,), in_...  39.4 us
    all_to_all x4, starting transfers between devices, exchange(): lax.all_to_all(value, 'expert', split_axis=0, concat_axis=0, tiled=True)  39 us
    pallas_call x4, Pallas kernels, half_product(): pl.pallas_call(half_kernel, grid_spec=pltpu.PrefetchScalarGridSpec(num_sc...  29.3 us
    pallas_call x2, Pallas kernels, pack(): pl.pallas_call(functools.partial(pack_kernel, part), grid=(experts // GRO...  12.7 us
    unnamed x14, local copies, waits for them, and re-layouts  5.32 us
  transfers between devices with their start and end apart: 6, of which 4 were waited for; matrix products, arithmetic and copies ran while one was open for 0% of the time, Pallas kernels for 33%

profile of v4, /device:TPU:50, one launch (start us, length us, event | category | flops | bytes accessed | tf_op | source)
XLA Modules:
  0.0 236.7 jit_solution(2938190746215455797)
XLA Ops:
  0.6 6.3 %pack_rows.2 = (bf16[64,288,128]{2,1,0:T(8,128)(2,1)}, f32[64,128]{1,0:T(8,128)}) custom-call(s32[8,128]{1,0:T(8,128)} %bitcast.10, bf16[8,128]{1,0:T(8,128)(2,1)} %bitcast.13, bf16[128,2048]{1,0:T(8,128)(2,1)} %x_ref.3, bf16[128,2048]{1,0:T(8,128)(2,1)} %dy_ref.3), custom_call_target="tpu_custom_call" | custom-call | flops 2147483648 | bytes 4718592 | tf_op jit(solution)/shard_map/pack_rows/pallas_call | solution.py:275
  7.0 11.1 %all-to-all-start.1 = ((bf16[64,288,128]{2,1,0:T(8,128)(2,1)}), bf16[64,288,128]{2,1,0:T(8,128)(2,1)}, u32[]{:S(2)}, u32[]{:S(2)}) async-start(bf16[64,288,128]{2,1,0:T(8,128)(2,1)} %get-tuple-element.34), calls=%async_computation.1 | async-start | bytes 9437184 | tf_op jit(solution)/shard_map/all_to_all | solution.py:373
  18.1 6.4 %pack_rows.3 = (bf16[64,288,128]{2,1,0:T(8,128)(2,1)}, f32[64,128]{1,0:T(8,128)}) custom-call(s32[8,128]{1,0:T(8,128)} %bitcast.11, bf16[8,128]{1,0:T(8,128)(2,1)} %bitcast.14, bf16[128,2048]{1,0:T(8,128)(2,1)} %x_ref.3, bf16[128,2048]{1,0:T(8,128)(2,1)} %dy_ref.3), custom_call_target="tpu_custom_call" | custom-call | flops 2147483648 | bytes 4718592 | tf_op jit(solution)/shard_map/pack_rows/pallas_call | solution.py:275
  24.4 55.0 %all-to-all-done.1.recv_ref = bf16[64,288,128]{2,1,0:T(8,128)(2,1)} async-done(((bf16[64,288,128]{2,1,0:T(8,128)(2,1)}), bf16[64,288,128]{2,1,0:T(8,128)(2,1)}, u32[]{:S(2)}, u32[]{:S(2)}) %all-to-all-start.1) | async-done | bytes 4718624 | tf_op jit(solution)/shard_map/all_to_all | solution.py:373
  79.5 8.3 %all-to-all-start = ((bf16[64,288,128]{2,1,0:T(8,128)(2,1)}), bf16[64,288,128]{2,1,0:T(8,128)(2,1)}, u32[]{:S(2)}, u32[]{:S(2)}) async-start(bf16[64,288,128]{2,1,0:T(8,128)(2,1)} %get-tuple-element.33), calls=%async_computation | async-start | bytes 9437184 | tf_op jit(solution)/shard_map/all_to_all | solution.py:373
  87.8 19.0 %expert.2 = (bf16[64,144,128]{2,1,0:T(8,128)(2,1)}, bf16[1152,2048]{1,0:T(8,128)(2,1)}, bf16[1152,2048]{1,0:T(8,128)(2,1)}, bf16[1152,1536]{1,0:T(8,128)(2,1)}, ...) custom-call(bf16[64,288,128]{2,1,0:T(8,128)(2,1)} %all-to-all-done.1.recv_ref, bf16[2048,768]{1,0:T(8,128)(2,1)} %bitcast.17, ...), custom_call_target="tpu_custom_call" | custom-call | flops 9059696640 | bytes 31457280 | tf_op jit(solution)/shard_map/expert/pallas_call | solution.py:300
  106.8 42.3 %all-to-all-done.recv_ref = bf16[64,288,128]{2,1,0:T(8,128)(2,1)} async-done(((bf16[64,288,128]{2,1,0:T(8,128)(2,1)}), bf16[64,288,128]{2,1,0:T(8,128)(2,1)}, u32[]{:S(2)}, u32[]{:S(2)}) %all-to-all-start) | async-done | bytes 4718624 | tf_op jit(solution)/shard_map/all_to_all | solution.py:373
  149.1 9.2 %all-to-all-start.3 = ((bf16[64,144,128]{2,1,0:T(8,128)(2,1)}), bf16[64,144,128]{2,1,0:T(8,128)(2,1)S(1)}, u32[]{:S(2)}, u32[]{:S(2)}) async-start(bf16[64,144,128]{2,1,0:T(8,128)(2,1)} %get-tuple-element.51), calls=%async_computation.3 | async-start | bytes 4718592 | tf_op jit(solution)/shard_map/all_to_all | solution.py:373
  158.3 20.4 %expert.3 = (bf16[64,160,128]{2,1,0:T(8,128)(2,1)}, bf16[1152,2048]{1,0:T(8,128)(2,1)}, bf16[1152,2048]{1,0:T(8,128)(2,1)}, bf16[1152,1536]{1,0:T(8,128)(2,1)}, bf16[1152,768]{1,0:T(8,128)(2,1)}) custom-call(bf16[64,288,128]{2,1,0:T(8,128)(2,1)} %all-to-all-done.recv_ref, ...), custom_call_target="tpu_custom_call", output_to_operand_aliasing={{1}: (5, {}), {2}: (6, {}), {3}: (7, {}), {4}: (8, {})} | custom-call | flops 9059696640 | bytes 31457280 | tf_op jit(solution)/shard_map/expert/pallas_call | solution.py:300
  178.7 8.2 %half_product.4 = bf16[1024,1536]{1,0:T(8,128)(2,1)} custom-call(s32[1]{0:T(128)S(6)} %sub.4.half_ref, bf16[1152,2048]{1,0:T(8,128)(2,1)} %get-tuple-element.43.left_ref, bf16[1152,1536]{1,0:T(8,128)(2,1)} %get-tuple-element.44.right_ref), custom_call_target="tpu_custom_call" | custom-call | flops 3623878656 | bytes 10485760 | tf_op jit(solution)/shard_map/half_product/pallas_call | solution.py:391
  186.9 0.0 collective-permute-start
  186.9 0.0 all-to-all-done.3.recv_ref
  186.9 0.0 copy-start
  186.9 1.4 copy-done
  188.4 10.3 %all-to-all-start.2 = ((bf16[64,160,128]{2,1,0:T(8,128)(2,1)}), bf16[64,160,128]{2,1,0:T(8,128)(2,1)S(1)}, u32[]{:S(2)}, u32[]{:S(2)}) async-start(bf16[64,160,128]{2,1,0:T(8,128)(2,1)} %get-tuple-element.42), calls=%async_computation.2 | async-start | bytes 5242880 | tf_op jit(solution)/shard_map/all_to_all | solution.py:373
  198.7 6.2 %half_product.6 = bf16[384,2048]{1,0:T(8,128)(2,1)} custom-call(s32[1]{0:T(128)S(6)} %sub.4.half_ref, bf16[1152,768]{1,0:T(8,128)(2,1)} %get-tuple-element.47.left_ref, bf16[1152,2048]{1,0:T(8,128)(2,1)} %get-tuple-element.48.right_ref), custom_call_target="tpu_custom_call" | custom-call | flops 1811939328 | bytes 10485760 | tf_op jit(solution)/shard_map/half_product/pallas_call | solution.py:391
  204.9 0.0 copy-start.4
  204.9 0.0 collective-permute-start.1
  204.9 3.7 %collective-permute-done.1.refs_0_ = bf16[384,2048]{1,0:T(8,128)(2,1)} collective-permute-done((bf16[384,2048]{1,0:T(8,128)(2,1)}, bf16[384,2048]{1,0:T(8,128)(2,1)}, u32[]{:S(2)}, u32[]{:S(2)}) %collective-permute-start.1) | collective-permute-done | bytes 1572896 | tf_op jit(solution)/shard_map/ppermute | solution.py:413
  208.6 6.5 %half_product.7 = bf16[384,2048]{1,0:T(8,128)(2,1)} custom-call(s32[1]{0:T(128)} %bitcast.5.half_ref, bf16[1152,768]{1,0:T(8,128)(2,1)} %get-tuple-element.47.left_ref, bf16[1152,2048]{1,0:T(8,128)(2,1)} %get-tuple-element.48.right_ref, bf16[384,2048]{1,0:T(8,128)(2,1)} %collective-permute-done.1.refs_0_), custom_call_target="tpu_custom_call" | custom-call | flops 1811939328 | bytes 10485760 | tf_op jit(solution)/shard_map/half_product/pallas_call | solution.py:391
  215.2 0.0 copy-done.4
  215.2 0.0 copy-start.1
  215.2 1.7 copy-done.1
  216.8 2.9 %first_sum.1.first_hbm = f32[128,2048]{1,0:T(8,128)S(1)} custom-call(bf16[64,144,128]{2,1,0:T(8,128)(2,1)S(1)} %copy-done.1, f32[64,128]{1,0:T(8,128)S(1)} %copy-done.4), custom_call_target="tpu_custom_call" | custom-call | flops 603979776 | bytes 2621440 | tf_op jit(solution)/shard_map/first_sum/pallas_call | solution.py:323
  219.8 0.0 copy-start.2
  219.8 1.0 copy-done.2
  220.7 0.0 copy-start.5
  220.7 0.0 copy-start.6
  220.7 0.0 collective-permute-done.refs_0_
  220.8 8.4 %half_product.5 = (bf16[1024,768]{1,0:T(8,128)(2,1)}, bf16[1024,768]{1,0:T(8,128)(2,1)}) custom-call(s32[1]{0:T(128)} %bitcast.5.half_ref, bf16[1152,2048]{1,0:T(8,128)(2,1)} %get-tuple-element.43.left_ref, bf16[1152,1536]{1,0:T(8,128)(2,1)} %get-tuple-element.44.right_ref, bf16[1024,1536]{1,0:T(8,128)(2,1)} %collective-permute-done.refs_0_), custom_call_target="tpu_custom_call" | custom-call | flops 3623878656 | bytes 10485760 | tf_op jit(solution)/shard_map/half_product/pallas_call | solution.py:391
  229.2 2.2 all-to-all-done.2.recv_ref
  231.4 0.0 copy-done.5
  231.4 0.0 copy-done.6
  231.4 0.0 copy-start.3
  231.4 1.2 copy-done.3
  232.6 4.0 %combine_parts.1 = (bf16[128,2048]{1,0:T(8,128)(2,1)}, bf16[8,128]{1,0:T(8,128)(2,1)}) custom-call(bf16[64,160,128]{2,1,0:T(8,128)(2,1)S(1)} %all-to-all-done.2.recv_ref, f32[64,128]{1,0:T(8,128)S(1)} %copy-done.4, f32[128,2048]{1,0:T(8,128)S(1)} %copy-done.3, s32[8,128]{1,0:T(8,128)S(1)} %bitcast.12, bf16[8,128]{1,0:T(8,128)(2,1)S(1)} %bitcast.15), custom_call_target="tpu_custom_call" | custom-call | flops 603979776 | bytes 2621440 | tf_op jit(solution)/shard_map/combine_parts/pallas_call | solution.py:342
Async XLA Ops:
  7.0 72.5 %all-to-all-start.1 = ((bf16[64,288,128]{2,1,0:T(8,128)(2,1)}), bf16[64,288,128]{2,1,0:T(8,128)(2,1)}, u32[]{:S(2)}, u32[]{:S(2)}) async-start(bf16[64,288,128]{2,1,0:T(8,128)(2,1)} %get-tuple-element.34), calls=%async_computation.1 | async-start | bytes 9437184 | tf_op jit(solution)/shard_map/all_to_all | solution.py:373
  79.5 69.6 %all-to-all-start = ((bf16[64,288,128]{2,1,0:T(8,128)(2,1)}), bf16[64,288,128]{2,1,0:T(8,128)(2,1)}, u32[]{:S(2)}, u32[]{:S(2)}) async-start(bf16[64,288,128]{2,1,0:T(8,128)(2,1)} %get-tuple-element.33), calls=%async_computation | async-start | bytes 9437184 | tf_op jit(solution)/shard_map/all_to_all | solution.py:373
  149.1 37.8 %all-to-all-start.3 = ((bf16[64,144,128]{2,1,0:T(8,128)(2,1)}), bf16[64,144,128]{2,1,0:T(8,128)(2,1)S(1)}, u32[]{:S(2)}, u32[]{:S(2)}) async-start(bf16[64,144,128]{2,1,0:T(8,128)(2,1)} %get-tuple-element.51), calls=%async_computation.3 | async-start | bytes 4718592 | tf_op jit(solution)/shard_map/all_to_all | solution.py:373
  186.9 33.9 %collective-permute-start = (bf16[1024,1536]{1,0:T(8,128)(2,1)}, bf16[1024,1536]{1,0:T(8,128)(2,1)}, u32[]{:S(2)}, u32[]{:S(2)}) collective-permute-start(bf16[1024,1536]{1,0:T(8,128)(2,1)} %half_product.4), channel_id=1, source_target_pairs={{0,64},{64,0},{1,65},{65,1},{2,66},{66,2},{3,67},{67,3},{4,68},{68... | collective-permute-start | bytes 9437192 | tf_op jit(solution)/shard_map/ppermute | solution.py:413
  186.9 1.5 copy-start
  188.4 43.0 %all-to-all-start.2 = ((bf16[64,160,128]{2,1,0:T(8,128)(2,1)}), bf16[64,160,128]{2,1,0:T(8,128)(2,1)S(1)}, u32[]{:S(2)}, u32[]{:S(2)}) async-start(bf16[64,160,128]{2,1,0:T(8,128)(2,1)} %get-tuple-element.42), calls=%async_computation.2 | async-start | bytes 5242880 | tf_op jit(solution)/shard_map/all_to_all | solution.py:373
  204.9 10.3 %copy-start.4 = (f32[64,128]{1,0:T(8,128)S(1)}, f32[64,128]{1,0:T(8,128)}, u32[]{:S(2)}) copy-start(f32[64,128]{1,0:T(8,128)} %get-tuple-element.50.rank_ref) | copy-start | bytes 98308
  204.9 3.8 %collective-permute-start.1 = (bf16[384,2048]{1,0:T(8,128)(2,1)}, bf16[384,2048]{1,0:T(8,128)(2,1)}, u32[]{:S(2)}, u32[]{:S(2)}) collective-permute-start(bf16[384,2048]{1,0:T(8,128)(2,1)} %half_product.6), channel_id=1, source_target_pairs={{0,64},{64,0},{1,65},{65,1},{2,66},{66,2},{3,67},{67,3},{4,68},{68... | collective-permute-start | bytes 4718600 | tf_op jit(solution)/shard_map/ppermute | solution.py:413
  215.2 1.7 copy-start.1
  219.8 1.0 copy-start.2
  220.7 10.6 %copy-start.5 = (s32[128,8]{0,1:T(8,128)S(1)}, s32[128,8]{0,1:T(8,128)}, u32[]{:S(2)}) copy-start(s32[128,8]{0,1:T(8,128)} %param.8) | copy-start | bytes 12292
  220.7 10.6 %copy-start.6 = (bf16[128,8]{0,1:T(8,128)(2,1)S(1)}, bf16[128,8]{0,1:T(8,128)(2,1)}, u32[]{:S(2)}) copy-start(bf16[128,8]{0,1:T(8,128)(2,1)} %param.9) | copy-start | bytes 6148
  231.4 1.2 copy-start.3
